TPU v7x, 256 devices: a whole 4x4x8 slice. The times are simulated.
256 devices in a mesh: ctx: 32 (over y, z), tp: 8 (over x, core).
Axes of the slice: x: 4, y: 4, z: 8, core: 2. Of those that a mesh axis runs over, the one named last changes fastest.
Arguments:
- tokens: bfloat16 [49152, 2048], P('ctx', 'tp')
- router: bfloat16 [2048], P('tp'), may hold values from -0.125 to 0.125
- gain: bfloat16 [2048], P('tp'), may hold values from 0.5 to 1.5
- w_query: bfloat16 [2048, 2048], P(None, 'tp')
- w_key: bfloat16 [2048, 2048], P(None, 'tp')
- w_value: bfloat16 [2048, 2048], P(None, 'tp'), may hold values from -0.125 to 0.125
- w_out: bfloat16 [2048, 2048], P('tp'), may hold values from -0.375 to 0.375
- counts: int32 [32], replicated, may hold values from 0 to 384, as said below
- picked: int32 [32, 384], replicated, may hold values from 0 to 49151, as said below
Outputs:
- update: bfloat16 [12288, 2048], P('ctx', 'tp')
Inputs may be any that keep to these rules, and one draw needn't show every extreme that they name: The counts sum to 6144; some index holds exactly 384. `picked`: row c holds distinct positions from c * 1536 to (c + 1) * 1536 - 1, in no particular order; only the first counts[c] entries are selected.
All inputs are finite; a program needn't handle non-finite values.
Results may differ from a plain program's by a relative error of at most 0.02.
Values may be sent and summed in bfloat16 or wider, within the bound.
A program may use at most 256 MiB of HBM per device.

v0:
```python
import math

import jax
import jax.numpy as jnp
from jax import lax
from jax.sharding import PartitionSpec as P

D = 2048
HD = 64


NEG_FILL = -1e30
EPSILON = 1e-05


def attend(carry_in, queries, places, key_block, value_block, key_places, head_count):
    running_max, running_sum, weighted = carry_in
    row_count = queries.shape[0]
    key_count = key_block.shape[0]
    query_3d = queries.reshape(row_count, head_count, HD)
    key_3d = key_block.reshape(key_count, head_count, HD)
    value_3d = value_block.reshape(key_count, head_count, HD)
    scores = jnp.einsum("qhd,khd->hqk", query_3d, key_3d, preferred_element_type=jnp.float32) * (
        1.0 / math.sqrt(HD)
    )
    allowed = key_places[None, None, :] <= places[None, :, None]
    scores = jnp.where(allowed, scores, NEG_FILL)
    new_max = jnp.maximum(running_max, jnp.max(scores, axis=2))
    weights = jnp.where(allowed, jnp.exp(scores - new_max[:, :, None]), 0.0)
    running_sum = jnp.sum(weights, axis=2)
    weighted = jnp.einsum(
        "hqk,khd->hqd", weights.astype(jnp.bfloat16), value_3d, preferred_element_type=jnp.float32
    )
    return (new_max, running_sum, weighted)


def guarded(carry_in, queries, places, key_block, value_block, key_places, head_count):

    def update_fn(carry_now):
        return attend(carry_now, queries, places, key_block, value_block, key_places, head_count)

    def keep_fn(carry_now):
        return carry_now

    return lax.cond(jnp.min(key_places) <= jnp.max(places), update_fn, keep_fn, carry_in)


def fresh_carry(row_count, head_count):
    return (
        jnp.full((head_count, row_count), NEG_FILL, jnp.float32),
        jnp.zeros((head_count, row_count), jnp.float32),
        jnp.zeros((head_count, row_count, HD), jnp.float32),
    )


def finish(carry_in):
    running_max, running_sum, weighted = carry_in
    safe_sum = jnp.where(running_sum > 0.0, running_sum, 1.0)
    result = (weighted / safe_sum[:, :, None]).astype(jnp.bfloat16)
    return result.transpose(1, 0, 2).reshape(result.shape[1], -1)


def local(tokens, router, gain, w_query, w_key, w_value, w_out, counts, picked):
    own_index = lax.axis_index("ctx")
    capacity = picked.shape[1]
    seq_local = tokens.shape[0]
    head_count = w_query.shape[1] // HD
    slot_ids = jnp.arange(capacity, dtype=jnp.int32)
    live_all = slot_ids[None, :] < counts[:, None]
    own_live = lax.dynamic_index_in_dim(live_all, own_index, 0, keepdims=False)
    own_picked = lax.dynamic_index_in_dim(picked, own_index, 0, keepdims=False)
    local_rows = jnp.take(tokens, own_picked - own_index * seq_local, axis=0)
    key_places = jnp.where(live_all, picked, jnp.int32(2**30)).reshape(-1)
    row_count = local_rows.shape[0]
    places = lax.dynamic_index_in_dim(picked, own_index, 0, keepdims=False)
    widened = local_rows.astype(jnp.float32)
    square_sum, route = lax.psum(
        (
            jnp.sum(widened * widened, axis=1),
            jnp.dot(local_rows, router, preferred_element_type=jnp.float32),
        ),
        "tp",
    )
    gating = jax.nn.sigmoid(route)
    norm_scale = lax.rsqrt(square_sum / D + EPSILON)
    normed = (widened * norm_scale[:, None] * gain.astype(jnp.float32)).astype(jnp.bfloat16)
    segment = lax.all_gather(normed, "tp", axis=1, tiled=True)
    query_sum, key_sum, value_sum = tuple(
        (
            jnp.dot(segment, matrix, preferred_element_type=jnp.float32)
            for matrix in (w_query, w_key, w_value)
        )
    )
    queries = query_sum.astype(jnp.bfloat16)
    key_rows = key_sum.astype(jnp.bfloat16)
    value_rows = value_sum.astype(jnp.bfloat16)
    segment = (
        lax.all_gather(key_rows, "ctx", axis=0, tiled=True),
        lax.all_gather(value_rows, "ctx", axis=0, tiled=True),
    )
    folded = guarded(
        fresh_carry(row_count, head_count),
        queries,
        places,
        segment[0],
        segment[1],
        key_places,
        head_count,
    )
    attended = finish(folded)
    partial_out = jnp.dot(attended, w_out, preferred_element_type=jnp.float32)
    summed = lax.psum_scatter(
        partial_out.astype(jnp.bfloat16), "tp", scatter_dimension=1, tiled=True
    ).astype(jnp.float32)
    gated = jnp.where(own_live[:, None], gating[:, None] * summed, 0.0).astype(jnp.bfloat16)
    return gated


def solution(mesh):
    return jax.shard_map(
        local,
        mesh=mesh,
        in_specs=(
            P("ctx", "tp"),
            P("tp"),
            P("tp"),
            P(None, "tp"),
            P(None, "tp"),
            P(None, "tp"),
            P("tp", None),
            P(),
            P(),
        ),
        out_specs=P("ctx", "tp"),
        check_vma=False,
    )
```

profile of v0, /device:TPU:1, one launch (start us, length us, event | category | flops | bytes accessed | tf_op | source)
XLA Modules:
  0.0 388.7 jit_solution(10093738145227559586)
XLA Ops:
  6.5 1.5 fusion.14
  8.0 0.7 fusion.12
  8.8 0.7 reshape.94
  9.4 2.9 gather_fusion
  12.3 0.2 fusion.9
  12.6 0.3 convolution_reduce_fusion
  12.8 15.0 %all-reduce = (f32[384]{0:T(512)S(1)}, f32[384]{0:T(512)S(1)}) all-reduce(f32[384]{0:T(512)S(1)} %fusion.9, f32[384]{0:T(512)S(1)} %convolution_reduce_fusion), channel_id=1, replica_groups=mesh['ctx'=32,'tp'=8] {'tp'}, use_global_device_ids=true, to_apply=%region_4.5 | all-reduce | flops 768 | bytes 6144 | tf_op jit(solution)/shard_map/psum | solution.py:77
  27.9 0.7 convert_element_type.38
  28.5 0.8 fusion.11
  29.4 0.0 all-gather.4.cloned.1.call-update
  29.4 0.0 all-gather.6.cloned.1.call-start
  29.5 29.1 %all-gather.4.cloned.1.call-done = bf16[384,2048]{1,0:T(8,128)(2,1)} async-done(((bf16[384,256]{1,0:T(8,128)(2,1)}), bf16[384,2048]{1,0:T(8,128)(2,1)}) %all-gather.4.cloned.1.call-update) | async-done | bytes 1572880 | tf_op jit(solution)/shard_map/all_gather | solution.py:87
  58.6 3.0 convolution_convert_fusion.2
  61.6 0.0 all-gather.8.cloned.1.call-start
  61.6 2.9 convolution_convert_fusion.1
  64.6 0.0 reduce-scatter.2.cloned.1.call-start
  64.6 1.6 fusion.15
  67.4 2.3 convolution_convert_fusion.3
  69.7 81.0 %all-gather.6.cloned.1.call-done = bf16[12288,256]{1,0:T(8,128)(2,1)} async-done(((bf16[384,256]{1,0:T(8,128)(2,1)}), bf16[12288,256]{1,0:T(8,128)(2,1)}) %all-gather.6.cloned.1.call-update) | async-done | bytes 6291472 | tf_op jit(solution)/shard_map/all_gather | solution.py:98
  150.7 88.3 %all-gather.8.cloned.1.call-done = bf16[12288,256]{1,0:T(8,128)(2,1)} async-done(((bf16[384,256]{1,0:T(8,128)(2,1)}), bf16[12288,256]{1,0:T(8,128)(2,1)}) %all-gather.8.cloned.1.call-update) | async-done | bytes 6291472 | tf_op jit(solution)/shard_map/all_gather | solution.py:99
  239.0 109.4 %conditional.1 = (f32[4,384]{1,0:T(4,128)S(1)}, f32[4,384,64]{1,2,0:T(8,128)S(1)}) conditional(s32[]{:T(128)} %convert_element_type.36, () %tuple.13, (s32[32,384]{1,0:T(8,128)S(1)}, s32[384]{0:T(512)S(1)}, bf16[384,256]{1,0:T(8,128)(2,1)S(1)}, bf16[12288,256]{1,0:T(8,128)(2,1)}, bf16[12288,256]{1,0:T(8,128)(2,1)}) %tuple.14), branch_computations={%region_5.6_spmd, %region_6.9_spmd} | conditional | flops 5081922048 | bytes 284284416 | solution.py:45
  239.0 5.1 %broadcast_compare_fusion = pred[384,12288]{1,0:T(8,128)(4,1)} fusion(s32[12288]{0:T(1024)S(1)} %le.27, s32[384]{0:T(512)S(1)} %get-tuple-element.16), kind=kLoop, calls=%fused_computation.8 | loop fusion | flops 4718592 | bytes 4769280 | tf_op jit(solution)/shard_map/cond/branch_1_fun/le | solution.py:26
  244.1 8.6 %copy.14 = bf16[12288,256]{0,1:T(8,128)(2,1)} copy(bf16[12288,256]{1,0:T(8,128)(2,1)} %get-tuple-element.32) | data formatting | bytes 12582912 | tf_op jit(solution)/shard_map
  252.8 0.2 copy.13
  252.9 30.4 %fusion = (f32[4,384]{1,0:T(4,128)S(1)}, f32[4,384,12288]{2,1,0:T(8,128)}) fusion(pred[384,12288]{1,0:T(8,128)(4,1)} %broadcast_compare_fusion, bf16[384,4,64]{0,2,1:T(8,128)(2,1)S(1)} %bitcast.23, bf16[12288,4,64]{0,2,1:T(8,128)(2,1)} %bitcast.20), kind=kOutput, calls=%fused_computation.3 | convolution fusion | flops 2472540672 | bytes 86710272 | tf_op jit(solution)/shard_map/cond/branch_1_fun/qhd,khd->hqk/dot_general | solution.py:23
  283.4 8.6 %copy.15 = bf16[12288,256]{0,1:T(8,128)(2,1)} copy(bf16[12288,256]{1,0:T(8,128)(2,1)} %get-tuple-element.33) | data formatting | bytes 12582912 | tf_op jit(solution)/shard_map
  292.0 30.8 %fusion.3 = f32[4,384,64]{1,2,0:T(8,128)S(1)} fusion(bf16[12288,4,64]{0,2,1:T(8,128)(2,1)} %bitcast.21, f32[4,384,12288]{2,1,0:T(8,128)} %get-tuple-element.41, f32[4,384]{1,0:T(4,128)S(1)} %broadcast_maximum_fusion, pred[384,12288]{1,0:T(8,128)(4,1)} %broadcast_compare_fusion), kind=kOutput, calls=%fused_computation.6 | convolution fusion | flops 2510290944 | bytes 86906880 | tf_op jit(solution)/shard_map/cond/branch_1_fun/hqk,khd->hqd/dot_general | solution.py:31
  322.9 25.5 %fusion.2 = f32[4,384]{1,0:T(4,128)S(1)} fusion(f32[4,384,12288]{2,1,0:T(8,128)} %get-tuple-element.41, f32[4,384]{1,0:T(4,128)S(1)} %broadcast_maximum_fusion, pred[384,12288]{1,0:T(8,128)(4,1)} %broadcast_compare_fusion), kind=kLoop, calls=%fused_computation.5 | loop fusion | flops 94370304 | bytes 80228352 | tf_op jit(solution)/shard_map/cond/branch_1_fun/reduce_sum | solution.py:30
  348.4 1.8 convolution_convert_fusion
  350.2 0.1 iota_compare_fusion
  350.3 30.1 %reduce-scatter.2.cloned.1.call-done = bf16[384,256]{1,0:T(8,128)(2,1)} async-done(((bf16[384,2048]{1,0:T(8,128)(2,1)}), bf16[384,256]{1,0:T(8,128)(2,1)}) %reduce-scatter.2.cloned.1.call-update) | async-done | bytes 196624 | tf_op jit(solution)/shard_map/reduce_scatter | solution.py:112
  380.4 1.8 select_convert_fusion
  (17 shorter events, 0.2 us)
Async XLA Ops:
  6.5 341.9 %copy-start = (bf16[256,2048]{1,0:T(8,128)(2,1)S(1)}, bf16[256,2048]{1,0:T(8,128)(2,1)}, u32[]{:S(2)}) copy-start(bf16[256,2048]{1,0:T(8,128)(2,1)} %param.17) | copy-start | bytes 3145732
  6.5 52.0 %all-gather.4.cloned.1.call-start = ((), (), s32[]{:S(2)}) async-start(), calls=%async_computation.1 | async-start | bytes 1769472 | tf_op jit(solution)/shard_map/all_gather | solution.py:87
  29.4 121.3 %all-gather.6.cloned.1.call-start = ((), (), s32[]{:S(2)}) async-start(), calls=%async_computation.2 | async-start | bytes 6488064 | tf_op jit(solution)/shard_map/all_gather | solution.py:98
  61.6 177.4 %all-gather.8.cloned.1.call-start = ((), (), s32[]{:S(2)}) async-start(), calls=%async_computation.3 | async-start | bytes 6488064 | tf_op jit(solution)/shard_map/all_gather | solution.py:99
  64.6 315.8 %reduce-scatter.2.cloned.1.call-start = ((), (), s32[]{:S(2)}) async-start(), calls=%async_computation.4 | async-start | bytes 1769472 | tf_op jit(solution)/shard_map/reduce_scatter | solution.py:112
  239.0 111.2 %copy-start.1 = (s32[32]{0:T(128)S(1)}, s32[32]{0:T(128)}, u32[]{:S(2)}) copy-start(s32[32]{0:T(128)} %param.18) | copy-start | bytes 388
Sparse Core Ops, SparseCore 0:
  29.5 29.0 all-gather.3
  61.7 88.9 all-gather.5
  153.3 85.6 all-gather.7
  350.3 30.0 reduce-scatter.1
where the time goes:
time: 391 us; the launch traced here: 389 us
  waiting for transfers between devices  229 us (59%)
  matrix products  71.5 us (18%)
  other arithmetic  38 us (10%)
  local copies, waits for them, and re-layouts  21.1 us (5%)
  blocking collectives  15 us (4%)
  between operations  14.5 us (4%)
    all_gather x1, waiting for transfers between devices, local(): lax.all_gather(value_rows, 'ctx', axis=0, tiled=True)  88.3 us
    all_gather x1, waiting for transfers between devices, local(): lax.all_gather(key_rows, 'ctx', axis=0, tiled=True)  81 us
    dot_general x1, matrix products, attend(): jnp.einsum('hqk,khd->hqd', weights.astype(jnp.bfloat16), value_3d, prefer...  30.8 us
    dot_general x1, matrix products, attend(): jnp.einsum('qhd,khd->hqk', query_3d, key_3d, preferred_element_type=jnp.f...  30.4 us
    reduce_scatter x1, waiting for transfers between devices, local(): lax.psum_scatter(partial_out.astype(jnp.bfloat16), 'tp', scatter_dimensio...  30.1 us
    all_gather x1, waiting for transfers between devices, local(): segment = lax.all_gather(normed, 'tp', axis=1, tiled=True)  29.1 us
    reduce_sum x1, other arithmetic, attend(): running_sum = jnp.sum(weights, axis=2)  25.5 us
    another operation x3, local copies, waits for them, and re-layouts  17.5 us
  transfers between devices with their start and end apart: 4, of which 4 were waited for; matrix products, arithmetic and copies ran while one was open for 2% of the time, Pallas kernels for 0%

commit v1 on v0

v1 whole, which is shorter than its diff:
```python
import functools
import math

import jax
import jax.numpy as jnp
from jax import lax
from jax.experimental import pallas as pl
from jax.experimental.pallas import tpu as pltpu
from jax.sharding import PartitionSpec as P

HD = 64
EPSILON = 1e-05
NEG_FILL = -1e30
MESH = pl.DeviceIdType.MESH
BF16 = jnp.bfloat16
F32 = jnp.float32
I32 = jnp.int32


def iota(shape, dim):
    return lax.broadcasted_iota(I32, shape, dim)


def one_hot(mask):
    return jnp.where(mask, 1.0, 0.0).astype(BF16)


def dot(a, b):
    return jnp.dot(a, b, preferred_element_type=F32)


def dot_t(a, b):
    return lax.dot_general(a, b, (((1,), (1,)), ((), ())), preferred_element_type=F32)


def remote(src, dst, send, recv, **where):
    return pltpu.make_async_remote_copy(
        src_ref=src, dst_ref=dst, send_sem=send, recv_sem=recv, device_id=where, device_id_type=MESH
    )


def kernel(
    cfg,
    counts_ref,
    picked_ref,
    tokens_ref,
    extra_ref,
    wq_hbm,
    wk_hbm,
    wv_hbm,
    wo_hbm,
    out_ref,
    wq_ref,
    wk_ref,
    wv_ref,
    wo_ref,
    row_send,
    row_recv,
    gathered,
    normed_ref,
    kv_send,
    kv_ref,
    q_send,
    q_recv,
    q_ref,
    max_ref,
    sum_ref,
    acc_ref,
    att_send,
    att_recv,
    pair_send,
    pair_recv,
    own_ref,
    part_send,
    part_recv,
    back_send,
    back_recv,
    w_sem,
    row_ss,
    row_rs,
    gat_ss,
    gat_rs,
    kvy_ss,
    kvy_rs,
    qy_ss,
    qy_rs,
    right_ss,
    right_rs,
    left_ss,
    left_rs,
    att_ss,
    att_rs,
    pair_ss,
    pair_rs,
    part_ss,
    part_rs,
    back_ss,
    back_rs,
):
    ny, nz, nx = cfg["ny"], cfg["nz"], cfg["nx"]
    rows, chunk, blocks = cfg["rows"], cfg["chunk"], cfg["blocks"]
    ctx, tp = ny * nz, nx * 2
    seq, feats = tokens_ref.shape
    cap = picked_ref.shape[1]
    slots = ctx * chunk
    half = rows // 2
    width = feats * tp

    c = lax.axis_index("ctx")
    t = lax.axis_index("tp")
    y, z = c // nz, lax.rem(c, nz)
    x, core = t // 2, lax.rem(t, 2)
    sibling = x * 2 + 1 - core

    barrier = pltpu.get_barrier_semaphore()

    def greet(i, _):
        pl.semaphore_signal(
            barrier, inc=1, device_id={"ctx": lax.rem(c + i, ctx)}, device_id_type=MESH
        )
        return 0

    lax.fori_loop(1, ctx, greet, 0)
    for dx in range(1, nx):
        pl.semaphore_signal(
            barrier,
            inc=1,
            device_id={"tp": lax.rem(x + dx, nx) * 2 + core},
            device_id_type=MESH,
        )
    pl.semaphore_signal(barrier, inc=1, device_id={"tp": sibling}, device_id_type=MESH)

    weight_copies = [
        pltpu.make_async_copy(src, dst, w_sem.at[i])
        for i, (src, dst) in enumerate(
            ((wq_hbm, wq_ref), (wk_hbm, wk_ref), (wv_hbm, wv_ref), (wo_hbm, wo_ref))
        )
    ]
    for copy in weight_copies:
        copy.start()

    own_count = counts_ref[c]
    own_offset = jnp.int32(0)
    for i in range(ctx):
        own_offset = own_offset + jnp.where(i < c, counts_ref[i], 0)
    place_row = picked_ref[pl.ds(c, 1), :] - c * seq
    place_full = jnp.broadcast_to(place_row, (cap, cap)).T
    live_row = iota((1, cap), 1) < own_count
    live_col = iota((cap, 1), 0) < own_count
    before_col = jnp.where(live_row & (place_row < place_full), 1.0, 0.0)
    before_row = jnp.where(live_col & (place_full < place_row), 1.0, 0.0)
    order_col = jnp.where(live_col, jnp.sum(before_col, axis=1, keepdims=True).astype(I32), -1)
    order_row = jnp.where(live_row, jnp.sum(before_row, axis=0, keepdims=True).astype(I32), -1)

    def wanted(index):
        dest, number = index // chunk, lax.rem(index, chunk)
        return ((dest - own_offset) & (ctx - 1)) + ctx * number

    deal = one_hot(wanted(iota((slots, cap), 0)) == order_row)
    undeal = one_hot(wanted(iota((cap, slots), 1)) == order_col)
    pick = one_hot(place_full[:, :1] == iota((cap, seq), 1))
    picked_rows = dot(pick, tokens_ref[...]).astype(BF16)
    row_send[...] = dot(deal, picked_rows).astype(BF16)

    pl.semaphore_wait(barrier, ctx - 1 + nx)

    def span(i):
        return pl.ds(pl.multiple_of(i * chunk, chunk), chunk)

    def exchange(send_ref, recv_ref, ss, rs):
        def begin(i, _):
            d = lax.rem(c + i, ctx)
            remote(
                send_ref.at[span(d)], recv_ref.at[span(c)], ss.at[d], rs.at[c], ctx=d
            ).start()
            return 0

        lax.fori_loop(1, ctx, begin, 0)
        recv_ref[span(c), :] = send_ref[span(c), :]

    def exchange_wait(send_ref, recv_ref, ss, rs):
        def end(i, _):
            d = lax.rem(c + i, ctx)
            remote(send_ref.at[span(d)], recv_ref.at[span(d)], ss.at[d], rs.at[d], ctx=d).wait()
            return 0

        lax.fori_loop(1, ctx, end, 0)

    exchange(row_send, row_recv, row_ss, row_rs)

    source = iota((8, slots), 1) // chunk
    offset_of = jnp.zeros((8, slots), I32)
    count_of = jnp.zeros((8, slots), I32)
    for i in range(ctx):
        count = counts_ref[i]
        offset_of = offset_of + jnp.where(source > i, count, 0)
        count_of = count_of + jnp.where(source == i, count, 0)
    number = ((c - offset_of) & (ctx - 1)) + ctx * lax.rem(iota((8, slots), 1), chunk)
    local_index = jnp.where(number < count_of, (offset_of + number - c) // ctx, -1)
    compact = one_hot(local_index[:1] == iota((rows, slots), 0))
    spread_index = jnp.broadcast_to(local_index[:1], (128, slots)).T[:, :1]
    spread = one_hot(spread_index == iota((slots, rows), 1))

    exchange_wait(row_send, row_recv, row_ss, row_rs)

    gathered[t, pl.ds(0, rows), :] = dot(compact, row_recv[...]).astype(BF16)
    gathered[t, pl.ds(rows, 16), :] = extra_ref[...]

    def gather_copy(block, slot, target):
        return remote(
            gathered.at[block], gathered.at[block], gat_ss.at[slot], gat_rs.at[block], tp=target
        )

    sends = []
    for dx in sorted(range(1, nx), key=lambda d: -min(d, nx - d)):
        sends.append(gather_copy(t, dx - 1, lax.rem(x + dx, nx) * 2 + core))
    sends.append(gather_copy(t, nx - 1, sibling))
    for copy in sends:
        copy.start()
    for dx in sorted(range(1, nx), key=lambda d: min(d, nx - d)):
        block = lax.rem(x + nx - dx, nx) * 2 + core
        gather_copy(block, nx - 1 + dx, sibling).wait_recv()
        onward = gather_copy(block, nx - 1 + dx, sibling)
        onward.start()
        sends.append(onward)
    for other in range(nx):
        gather_copy(other * 2 + 1 - core, 0, sibling).wait_recv()
    for copy in sends:
        copy.wait_send()

    squares = jnp.zeros((rows, feats), F32)
    routes = jnp.zeros((rows, feats), F32)
    for b in range(tp):
        wide = gathered[b, pl.ds(0, rows), :].astype(F32)
        params = gathered[b, pl.ds(rows, 16), :].astype(F32)
        squares = squares + wide * wide
        routes = routes + wide * params[1:2]
    scale = lax.rsqrt(jnp.sum(squares, axis=1, keepdims=True) / width + EPSILON)
    gating = 1.0 / (1.0 + jnp.exp(-jnp.sum(routes, axis=1, keepdims=True)))
    for b in range(tp):
        wide = gathered[b, pl.ds(0, rows), :].astype(F32)
        params = gathered[b, pl.ds(rows, 16), :].astype(F32)
        normed_ref[:, pl.ds(b * feats, feats)] = (wide * scale * params[0:1]).astype(BF16)

    for copy in weight_copies:
        copy.wait()
    normed = normed_ref[...]
    keys = dot(normed, wk_ref[...]).astype(BF16)
    values = dot(normed, wv_ref[...]).astype(BF16)
    for h in range(ny):
        cols = slice(h * HD, (h + 1) * HD)
        kv_send[h] = jnp.concatenate([keys[:, cols], values[:, cols]], axis=1)

    def across_y(send_ref, target, recv_slot, ss, rs, dy):
        other = lax.rem(y + dy, ny)
        return remote(send_ref.at[other], target(recv_slot), ss.at[dy], rs.at[recv_slot], ctx=other * nz + z)

    steps = sorted(range(1, ny), key=lambda d: -min(d, ny - d))
    kv_slot = lambda s: kv_ref.at[z, s]
    q_slot = lambda s: q_recv.at[s]
    att_slot = lambda s: att_recv.at[s]
    for dy in steps:
        across_y(kv_send, kv_slot, y, kvy_ss, kvy_rs, dy).start()
    kv_ref[z, y] = kv_send[y]

    queries = (dot(normed, wq_ref[...]).astype(BF16).astype(F32) * (1.0 / math.sqrt(HD))).astype(BF16)
    for h in range(ny):
        cols = slice(h * HD, (h + 1) * HD)
        q_send[h] = jnp.concatenate([queries[:half, cols], queries[half:, cols]], axis=1)
    for dy in steps:
        across_y(q_send, q_slot, y, qy_ss, qy_rs, dy).start()
    q_recv[y] = q_send[y]

    right = y * nz + lax.rem(z + 1, nz)
    left = y * nz + lax.rem(z + nz - 1, nz)
    far = nz // 2

    def ring_copy(to_right, step, slab):
        if to_right:
            origin = lax.rem(z + nz - step, nz)
            ss, rs, target = right_ss, right_rs, right
        else:
            origin = lax.rem(z + step, nz)
            ss, rs, target = left_ss, left_rs, left
        view = kv_ref.at[origin, slab]
        return remote(view, view, ss.at[step, slab], rs.at[step, slab], ctx=target)

    def hops(to_right, slab):
        return far if (slab < ny // 2) == to_right else far - 1

    ring_sends = []

    def forward(step, slab, to_right):
        if step < hops(to_right, slab):
            copy = ring_copy(to_right, step, slab)
            copy.start()
            ring_sends.append(copy)

    def arrived(step, slab, to_right):
        if step <= hops(to_right, slab):
            view = kv_ref.at[lax.rem(z + (nz - step if to_right else step), nz), slab]
            ss, rs = (right_ss, right_rs) if to_right else (left_ss, left_rs)
            remote(
                view, view, ss.at[step - 1, slab], rs.at[step - 1, slab], ctx=right if to_right else left
            ).wait_recv()

    for dy in range(1, ny):
        other = lax.rem(y + dy, ny)
        remote(
            kv_send.at[other], kv_ref.at[z, other], kvy_ss.at[dy], kvy_rs.at[other], ctx=other * nz + z
        ).wait()
    for slab in range(ny):
        for to_right in (True, False):
            forward(0, slab, to_right)
    for dy in range(1, ny):
        other = lax.rem(y + dy, ny)
        remote(
            q_send.at[other], q_recv.at[other], qy_ss.at[dy], qy_rs.at[other], ctx=other * nz + z
        ).wait()

    zeros = jnp.zeros((half, HD), BF16)
    for s in range(ny):
        packed = q_recv[s]
        q_ref[s, pl.ds(0, half), :] = jnp.concatenate([packed[:, :HD], zeros], axis=1)
        q_ref[s, pl.ds(half, half), :] = jnp.concatenate([packed[:, HD:], zeros], axis=1)

    size = rows // blocks
    tile = ny * size
    tile_row = iota((tile, 1), 0)
    tile_col = iota((1, tile), 1)
    query_key = lax.rem(tile_row, size) * ctx + (tile_row // size) * nz + z
    key_base = lax.rem(tile_col, size) * ctx + (tile_col // size) * nz

    def attend(origin, first):
        allowed = key_base + origin <= query_key
        for b in range(blocks):
            q = q_ref[:, pl.ds(b * size, size), :].reshape(tile, 2 * HD)
            near = kv_ref[origin, :, pl.ds(b * size, size), :].reshape(tile, 2 * HD)
            near_score = jnp.where(allowed, dot_t(q, near), NEG_FILL)
            peak = jnp.max(near_score, axis=1, keepdims=True)
            if b:
                past = kv_ref[origin, :, pl.ds(0, b * size), :].reshape(b * tile, 2 * HD)
                past_score = dot_t(q, past)
                peak = jnp.maximum(peak, jnp.max(past_score, axis=1, keepdims=True))
            if not first:
                old = max_ref[b]
                peak = jnp.maximum(old, peak)
                shrink = jnp.exp(old - peak)
            near_weight = jnp.where(allowed, jnp.exp(near_score - peak), 0.0)
            total = jnp.sum(near_weight, axis=1, keepdims=True)
            product = dot(near_weight.astype(BF16), near)
            if b:
                past_weight = jnp.exp(past_score - peak)
                total = total + jnp.sum(past_weight, axis=1, keepdims=True)
                product = product + dot(past_weight.astype(BF16), past)
            if not first:
                total = total + sum_ref[b] * shrink
                product = product + acc_ref[b] * shrink
            max_ref[b] = peak
            sum_ref[b] = total
            acc_ref[b] = product

    attend(z, True)
    for step in range(1, far + 1):
        for slab in range(ny):
            for to_right in (True, False):
                arrived(step, slab, to_right)
                forward(step, slab, to_right)
        if step < far:

            def both(i, _):
                attend(lax.rem(z + jnp.where(i == 0, nz - step, step), nz), False)
                return 0

            lax.fori_loop(0, 2, both, 0)
        else:
            attend(lax.rem(z + far, nz), False)
    for copy in ring_sends:
        copy.wait_send()

    for b in range(blocks):
        result = (acc_ref[b] / sum_ref[b]).astype(BF16).reshape(ny, size, 2 * HD)
        q_ref[:, pl.ds(b * size, size), :] = result
    for s in range(ny):
        att_send[s] = jnp.concatenate(
            [q_ref[s, pl.ds(0, half), :][:, HD:], q_ref[s, pl.ds(half, half), :][:, HD:]], axis=1
        )
    for dy in steps:
        across_y(att_send, att_slot, y, att_ss, att_rs, dy).start()
    att_recv[y] = att_send[y]
    for dy in range(1, ny):
        other = lax.rem(y + dy, ny)
        remote(
            att_send.at[other], att_recv.at[other], att_ss.at[dy], att_rs.at[other], ctx=other * nz + z
        ).wait()
    joined = [att_recv[h] for h in range(ny)]
    attended = jnp.concatenate(
        [
            jnp.concatenate([packed[:, :HD] for packed in joined], axis=1),
            jnp.concatenate([packed[:, HD:] for packed in joined], axis=1),
        ],
        axis=0,
    )

    def columns(index):
        return pl.ds(pl.multiple_of(index * feats, feats), feats)

    pair_copies = []
    for dx in range(nx):
        other = lax.rem(x + dx, nx)
        pair_send[dx] = dot(attended, wo_ref[:, columns(other * 2 + 1 - core)]).astype(BF16)
        copy = remote(pair_send.at[dx], pair_recv.at[dx], pair_ss.at[dx], pair_rs.at[dx], tp=sibling)
        copy.start()
        pair_copies.append(copy)
    for dx in range(nx):
        other = lax.rem(x + dx, nx)
        own_ref[dx] = dot(attended, wo_ref[:, columns(other * 2 + core)])
    part_copies = []
    for dx in sorted(range(1, nx), key=lambda d: -min(d, nx - d)):
        other = lax.rem(x + dx, nx)
        pair_copies[dx].wait()
        part_send[dx] = (own_ref[dx] + pair_recv[dx].astype(F32)).astype(BF16)
        copy = remote(
            part_send.at[dx], part_recv.at[dx], part_ss.at[dx], part_rs.at[dx], tp=other * 2 + core
        )
        copy.start()
        part_copies.append(copy)
    pair_copies[0].wait()
    projected = own_ref[0] + pair_recv[0].astype(F32)
    for copy in part_copies:
        copy.wait()
    for dx in range(1, nx):
        projected = projected + part_recv[dx].astype(F32)
    gated = (gating * projected).astype(BF16)

    back_send[...] = dot(spread, gated).astype(BF16)
    exchange(back_send, back_recv, back_ss, back_rs)
    exchange_wait(back_send, back_recv, back_ss, back_rs)
    out_ref[...] = dot(undeal, back_recv[...]).astype(BF16)


def build(cfg, tokens, router, gain, w_query, w_key, w_value, w_out, counts, picked):
    ny, nz, nx = cfg["ny"], cfg["nz"], cfg["nx"]
    rows, chunk, blocks = cfg["rows"], cfg["chunk"], cfg["blocks"]
    ctx, tp = ny * nz, nx * 2
    feats = tokens.shape[1]
    cap = picked.shape[1]
    slots = ctx * chunk
    half = rows // 2
    width = feats * tp
    tile = ny * rows // blocks
    far = nz // 2
    extra = jnp.concatenate([gain[None], router[None], jnp.zeros((14, feats), BF16)], axis=0)
    vmem = pl.BlockSpec(memory_space=pltpu.VMEM)
    hbm = pl.BlockSpec(memory_space=pl.ANY)
    dma = pltpu.SemaphoreType.DMA
    return pl.pallas_call(
        functools.partial(kernel, cfg),
        out_shape=jax.ShapeDtypeStruct((cap, feats), BF16),
        in_specs=[pl.BlockSpec(memory_space=pltpu.SMEM), vmem, vmem, vmem, hbm, hbm, hbm, hbm],
        out_specs=vmem,
        scratch_shapes=[
            pltpu.VMEM((width, feats), BF16),
            pltpu.VMEM((width, feats), BF16),
            pltpu.VMEM((width, feats), BF16),
            pltpu.VMEM((feats, width), BF16),
            pltpu.VMEM((slots, feats), BF16),
            pltpu.VMEM((slots, feats), BF16),
            pltpu.VMEM((tp, rows + 16, feats), BF16),
            pltpu.VMEM((rows, width), BF16),
            pltpu.VMEM((ny, rows, 2 * HD), BF16),
            pltpu.VMEM((nz, ny, rows, 2 * HD), BF16),
            pltpu.VMEM((ny, half, 2 * HD), BF16),
            pltpu.VMEM((ny, half, 2 * HD), BF16),
            pltpu.VMEM((ny, rows, 2 * HD), BF16),
            pltpu.VMEM((blocks, tile, 1), F32),
            pltpu.VMEM((blocks, tile, 1), F32),
            pltpu.VMEM((blocks, tile, 2 * HD), F32),
            pltpu.VMEM((ny, half, 2 * HD), BF16),
            pltpu.VMEM((ny, half, 2 * HD), BF16),
            pltpu.VMEM((nx, rows, feats), BF16),
            pltpu.VMEM((nx, rows, feats), BF16),
            pltpu.VMEM((nx, rows, feats), F32),
            pltpu.VMEM((nx, rows, feats), BF16),
            pltpu.VMEM((nx, rows, feats), BF16),
            pltpu.VMEM((slots, feats), BF16),
            pltpu.VMEM((slots, feats), BF16),
            dma((4,)),
            dma((ctx,)),
            dma((ctx,)),
            dma((2 * nx,)),
            dma((tp,)),
            dma((ny,)),
            dma((ny,)),
            dma((ny,)),
            dma((ny,)),
            dma((far, ny)),
            dma((far, ny)),
            dma((far, ny)),
            dma((far, ny)),
            dma((ny,)),
            dma((ny,)),
            dma((nx,)),
            dma((nx,)),
            dma((nx,)),
            dma((nx,)),
            dma((ctx,)),
            dma((ctx,)),
        ],
        compiler_params=pltpu.CompilerParams(
            collective_id=0, has_side_effects=True, vmem_limit_bytes=48 * 1024 * 1024
        ),
    )(counts, picked, tokens, extra, w_query, w_key, w_value, w_out)


def solution(mesh, nz=8, selected=6144, cap=384, blocks=3):
    ctx, tp = mesh.shape["ctx"], mesh.shape["tp"]
    per = -(-cap // ctx)
    cfg = {
        "ny": ctx // nz,
        "nz": nz,
        "nx": tp // 2,
        "rows": selected // ctx,
        "chunk": -(-per // 16) * 16,
        "blocks": blocks,
    }
    return jax.shard_map(
        functools.partial(build, cfg),
        mesh=mesh,
        in_specs=(
            P("ctx", "tp"),
            P("tp"),
            P("tp"),
            P(None, "tp"),
            P(None, "tp"),
            P(None, "tp"),
            P("tp", None),
            P(),
            P(),
        ),
        out_specs=P("ctx", "tp"),
        check_vma=False,
    )
```

time: 391 us -> 89.6 us (0.23)
  waiting for transfers between devices: 229 us -> 0 us
  Pallas kernels: 0 us -> 79.7 us
  matrix products: 71.5 us -> 0 us
  other arithmetic: 38 us -> 0.08 us
  blocking collectives: 15 us -> 0 us
  between operations: 14.5 us -> 0.02 us
  local copies, waits for them, and re-layouts: 21.1 us -> 9.4 us
    all_gather x3 -> x0, waiting for transfers between devices: 198 us -> none  [the longest x1 88.3 us: local(): lax.all_gather(value_rows, 'ctx', axis=0, tiled=True)]
    pallas_call x0 -> x1, Pallas kernels: none -> 79.7 us  [build(): pl.pallas_call(functools.partial(kernel, cfg), out_shape=jax.ShapeDtypeSt...]
    dot_general x7 -> x0, matrix products: 71.5 us -> none  [the longest x1 30.8 us: attend(): jnp.einsum('hqk,khd->hqd', weights.astype(jnp.bfloat16), value_3d, prefer...]
    reduce_scatter x1 -> x0, waiting for transfers between devices: 30.1 us -> none  [local(): lax.psum_scatter(partial_out.astype(jnp.bfloat16), 'tp', scatter_dimensio...]
    reduce_sum x2 -> x0, other arithmetic: 25.7 us -> none  [the longest x1 25.5 us: attend(): running_sum = jnp.sum(weights, axis=2)]
    another operation x3 -> x0, local copies, waits for them, and re-layouts: 17.5 us -> none
    psum x1 -> x0, blocking collectives: 15 us -> none  [local(): lax.psum((jnp.sum(widened * widened, axis=1), jnp.dot(local_rows, router,...]
    unnamed x5 -> x19, local copies, waits for them, and re-layouts: 0.67 us -> 9.31 us
  transfers between devices with their start and end apart: 4 -> 0, of which waited for: 4 -> 0; matrix products, arithmetic and copies ran while one was open for 2% -> 0% of each run, Pallas kernels for 0% -> 0%
where the time goes in v1:
time: 89.6 us; the launch traced here: 89.2 us
  Pallas kernels  79.7 us (89%)
  local copies, waits for them, and re-layouts  9.4 us (10%)
    pallas_call x1, Pallas kernels, build(): pl.pallas_call(functools.partial(kernel, cfg), out_shape=jax.ShapeDtypeSt...  79.7 us
    unnamed x19, local copies, waits for them, and re-layouts  9.31 us

profile of v1, /device:TPU:1, one launch (start us, length us, event | category | flops | bytes accessed | tf_op | source)
XLA Modules:
  0.0 89.2 jit_solution(14400969357998495456)
XLA Ops:
  0.0 0.0 copy-start.7
  0.0 0.1 pad.2.clone
  0.1 0.6 copy-done.7
  0.7 0.0 copy-start.8
  0.7 0.6 copy-done.8
  1.3 0.0 copy-start.6
  1.3 0.1 maximum_maximum_fusion.extra_ref
  1.4 0.6 copy-done.6
  2.0 0.0 copy-start
  2.0 1.2 %copy-done = bf16[2048,256]{1,0:T(8,128)(2,1)S(1)} copy-done((bf16[2048,256]{1,0:T(8,128)(2,1)S(1)}, bf16[2048,256]{1,0:T(8,128)(2,1)}, u32[]{:S(2)}) %copy-start) | copy-done | bytes 1048600
  3.2 0.0 copy-start.1
  3.2 1.2 %copy-done.1 = bf16[2048,256]{1,0:T(8,128)(2,1)S(1)} copy-done((bf16[2048,256]{1,0:T(8,128)(2,1)S(1)}, bf16[2048,256]{1,0:T(8,128)(2,1)}, u32[]{:S(2)}) %copy-start.1) | copy-done | bytes 1048600
  4.4 0.0 copy-start.2
  4.4 1.2 %copy-done.2 = bf16[2048,256]{1,0:T(8,128)(2,1)S(1)} copy-done((bf16[2048,256]{1,0:T(8,128)(2,1)S(1)}, bf16[2048,256]{1,0:T(8,128)(2,1)}, u32[]{:S(2)}) %copy-start.2) | copy-done | bytes 1048600
  5.7 0.0 copy-start.3
  5.7 1.2 %copy-done.3 = bf16[256,2048]{1,0:T(8,128)(2,1)S(1)} copy-done((bf16[256,2048]{1,0:T(8,128)(2,1)S(1)}, bf16[256,2048]{1,0:T(8,128)(2,1)}, u32[]{:S(2)}) %copy-start.3) | copy-done | bytes 1048600
  6.9 0.0 copy-start.4
  6.9 1.1 %copy-done.4 = bf16[1536,256]{1,0:T(8,128)(2,1)S(1)} copy-done((bf16[1536,256]{1,0:T(8,128)(2,1)S(1)}, bf16[1536,256]{1,0:T(8,128)(2,1)}, u32[]{:S(2)}) %copy-start.4) | copy-done | bytes 786456
  8.0 0.0 copy-start.5
  8.0 0.8 copy-done.5
  8.8 79.7 %shard_map.91 = bf16[384,256]{1,0:T(8,128)(2,1)S(1)} custom-call(s32[32]{0:T(128)S(1)} %copy-done.6, s32[32,384]{1,0:T(8,128)S(1)} %copy-done.5, bf16[1536,256]{1,0:T(8,128)(2,1)S(1)} %copy-done.4, bf16[16,256]{1,0:T(8,128)(2,1)S(1)} %maximum_maximum_fusion.extra_ref, bf16[2048,256]{1,0:T(8,128)(2,1)S(1)} %copy-done, bf16[2048,256]{1,0:T(8,128)(2,1)S(1)} %copy-done.1, ...), custom_call_target="tpu_custom_call" | custom-call | tf_op jit(solution)/shard_map/pallas_call | solution.py:457
  88.6 0.7 copy.11
  (3 shorter events, 0.0 us)
Async XLA Ops:
  0.0 0.7 copy-start.7
  0.7 0.7 copy-start.8
  1.3 0.7 copy-start.6
  2.0 1.2 %copy-start = (bf16[2048,256]{1,0:T(8,128)(2,1)S(1)}, bf16[2048,256]{1,0:T(8,128)(2,1)}, u32[]{:S(2)}) copy-start(bf16[2048,256]{1,0:T(8,128)(2,1)} %wq_hbm.1) | copy-start | bytes 3145732
  3.2 1.2 %copy-start.1 = (bf16[2048,256]{1,0:T(8,128)(2,1)S(1)}, bf16[2048,256]{1,0:T(8,128)(2,1)}, u32[]{:S(2)}) copy-start(bf16[2048,256]{1,0:T(8,128)(2,1)} %wk_hbm.1) | copy-start | bytes 3145732
  4.4 1.2 %copy-start.2 = (bf16[2048,256]{1,0:T(8,128)(2,1)S(1)}, bf16[2048,256]{1,0:T(8,128)(2,1)}, u32[]{:S(2)}) copy-start(bf16[2048,256]{1,0:T(8,128)(2,1)} %wv_hbm.1) | copy-start | bytes 3145732
  5.7 1.2 %copy-start.3 = (bf16[256,2048]{1,0:T(8,128)(2,1)S(1)}, bf16[256,2048]{1,0:T(8,128)(2,1)}, u32[]{:S(2)}) copy-start(bf16[256,2048]{1,0:T(8,128)(2,1)} %wo_hbm.1) | copy-start | bytes 3145732
  6.9 1.1 %copy-start.4 = (bf16[1536,256]{1,0:T(8,128)(2,1)S(1)}, bf16[1536,256]{1,0:T(8,128)(2,1)}, u32[]{:S(2)}) copy-start(bf16[1536,256]{1,0:T(8,128)(2,1)} %tokens_ref.1) | copy-start | bytes 2359300
  8.0 0.8 copy-start.5

commit v2 on v1

v2 whole, which is shorter than its diff:
```python
import functools
import math

import jax
import jax.numpy as jnp
from jax import lax
from jax.experimental import pallas as pl
from jax.experimental.pallas import tpu as pltpu
from jax.sharding import PartitionSpec as P

HD = 64
EPSILON = 1e-05
NEG_FILL = -1e30
MESH = pl.DeviceIdType.MESH
BF16 = jnp.bfloat16
F32 = jnp.float32
I32 = jnp.int32
VMEM_BYTES = 60 * 1024 * 1024


def iota(shape, dim):
    return lax.broadcasted_iota(I32, shape, dim)


def one_hot(mask):
    return jnp.where(mask, 1.0, 0.0).astype(BF16)


def dot(a, b):
    return jnp.dot(a, b, preferred_element_type=F32)


def dot_t(a, b):
    return lax.dot_general(a, b, (((1,), (1,)), ((), ())), preferred_element_type=F32)


def remote(src, dst, send, recv, **where):
    return pltpu.make_async_remote_copy(
        src_ref=src, dst_ref=dst, send_sem=send, recv_sem=recv, device_id=where, device_id_type=MESH
    )


class RingGather:
    def __init__(self, n, pos, core, view, ss, rs, device, sibling, parts=2):
        self.n, self.pos, self.core, self.view, self.ss, self.rs = n, pos, core, view, ss, rs
        self.device, self.sibling, self.parts = device, sibling, parts
        self.sent = []

    def at(self, step):
        return lax.rem(self.pos + step + self.n, self.n)

    def copy(self, pos, which, part, target):
        view = self.view(pos, which, part)
        return remote(view, view, self.ss.at[len(self.sent)], self.rs.at[pos, which, part], **target)

    def send(self, pos, part, target):
        copy = self.copy(pos, self.core, part, target)
        copy.start()
        self.sent.append(copy)

    def wait(self, pos, which, part):
        view = self.view(pos, which, part)
        remote(view, view, self.ss.at[0], self.rs.at[pos, which, part], **self.sibling).wait_recv()

    def start(self):
        right, left = self.device(self.at(1)), self.device(self.at(-1))
        parts = range(self.parts)
        for part in parts:
            if self.n > 1:
                self.send(self.pos, part, right)
            if self.n > 2:
                self.send(self.pos, self.parts - 1 - part, left)
        for part in parts:
            self.send(self.pos, part, self.sibling)

    def near(self):
        if self.n == 1:
            return
        right, left = self.device(self.at(1)), self.device(self.at(-1))
        for turn in range(self.parts):
            for step in (-1, 1) if self.n > 2 else (-1,):
                part = turn if step == -1 else self.parts - 1 - turn
                self.wait(self.at(step), self.core, part)
                if self.n > 2 and (turn == 0 and self.parts == 2 or self.parts == 1 and step == -1):
                    self.send(self.at(step), part, right if step == -1 else left)
                self.send(self.at(step), part, self.sibling)

    def far(self):
        if self.n > 2:
            for part in range(self.parts):
                self.wait(self.at(2), self.core, part)
                self.send(self.at(2), part, self.sibling)

    def from_sibling(self, pos):
        for part in range(self.parts):
            self.wait(pos, 1 - self.core, part)

    def finish(self):
        for copy in self.sent:
            copy.wait_send()


class Gather:
    def __init__(self, n, pos, core, view, ss, rs, device, sibling):
        self.n, self.pos, self.core, self.view, self.ss, self.rs = n, pos, core, view, ss, rs
        self.device, self.sibling = device, sibling
        self.sent = []

    def at(self, step):
        return lax.rem(self.pos + step, self.n)

    def copy(self, pos, which, slot, target):
        view = self.view(pos, which)
        return remote(view, view, self.ss.at[slot], self.rs.at[pos, which], **target)

    def send(self, pos, target):
        copy = self.copy(pos, self.core, len(self.sent), target)
        copy.start()
        self.sent.append(copy)

    def steps(self):
        return sorted(range(1, self.n), key=lambda d: min(d, self.n - d))

    def start(self):
        self.send(self.pos, self.sibling)
        for step in self.steps():
            self.send(self.pos, self.device(self.at(step)))

    def pass_on(self, step):
        self.copy(self.at(step), self.core, 0, self.sibling).wait_recv()
        self.send(self.at(step), self.sibling)

    def from_sibling(self, pos):
        self.copy(pos, 1 - self.core, 0, self.sibling).wait_recv()

    def finish(self):
        for copy in self.sent:
            copy.wait_send()


def kernel(
    cfg,
    counts_ref,
    gain_ref,
    router_ref,
    picked_hbm,
    tokens_hbm,
    wq_hbm,
    wk_hbm,
    wv_hbm,
    wo_hbm,
    out_ref,
    picked_ref,
    tokens_ref,
    wq_ref,
    wk_ref,
    wv_ref,
    wo_ref,
    row_send,
    row_recv,
    gathered,
    normed_ref,
    kv_send,
    kv_ref,
    q_send,
    q_recv,
    q_ref,
    value_ref,
    max_ref,
    acc_ref,
    att_send,
    att_recv,
    pair_send,
    pair_recv,
    own_ref,
    part_send,
    part_recv,
    back_send,
    back_recv,
    w_sem,
    row_ss,
    row_rs,
    gat_ss,
    gat_rs,
    kvz_ss,
    kvz_rs,
    qz_ss,
    qz_rs,
    kvy_ss,
    kvy_rs,
    att_ss,
    att_rs,
    pair_ss,
    pair_rs,
    part_ss,
    part_rs,
    back_ss,
    back_rs,
):
    ny, nz, nx = cfg["ny"], cfg["nz"], cfg["nx"]
    rows, chunk, blocks = cfg["rows"], cfg["chunk"], cfg["blocks"]
    ctx, tp = ny * nz, nx * 2
    seq, feats = tokens_ref.shape
    cap = picked_ref.shape[1]
    slots = ctx * chunk
    shift = chunk.bit_length() - 1
    half = rows // 2
    width = feats * tp
    heads = feats // HD
    zs = nz // 2

    loads = [
        pltpu.make_async_copy(src, dst, w_sem.at[i])
        for i, (src, dst) in enumerate(
            (
                (picked_hbm, picked_ref),
                (tokens_hbm, tokens_ref),
                (wk_hbm, wk_ref),
                (wv_hbm, wv_ref),
                (wq_hbm, wq_ref),
                (wo_hbm, wo_ref),
            )
        )
    ]
    for copy in loads:
        copy.start()

    c = lax.axis_index("ctx")
    t = lax.axis_index("tp")
    y, z = c // nz, lax.rem(c, nz)
    x, core = t // 2, lax.rem(t, 2)
    sibling = x * 2 + 1 - core

    barrier = pltpu.get_barrier_semaphore()

    def greet(i, _):
        pl.semaphore_signal(
            barrier, inc=1, device_id={"ctx": lax.rem(c + i, ctx)}, device_id_type=MESH
        )
        return 0

    lax.fori_loop(1, ctx, greet, 0)
    for dx in range(1, nx):
        pl.semaphore_signal(
            barrier,
            inc=1,
            device_id={"tp": lax.rem(x + dx, nx) * 2 + core},
            device_id_type=MESH,
        )
    pl.semaphore_signal(barrier, inc=1, device_id={"tp": sibling}, device_id_type=MESH)
    for dz in range(1, nz):
        pl.semaphore_signal(
            barrier,
            inc=1,
            device_id={"ctx": y * nz + lax.rem(z + dz, nz), "tp": sibling},
            device_id_type=MESH,
        )

    own_count = counts_ref[c]
    own_offset = jnp.int32(0)
    for i in range(ctx):
        own_offset = own_offset + jnp.where(i < c, counts_ref[i], 0)
    loads[0].wait()
    place_row = picked_ref[pl.ds(c, 1), :] - c * seq
    place_col = jnp.broadcast_to(place_row, (8, cap)).T[:, :1]
    live_row = iota((1, cap), 1) < own_count
    live_col = iota((cap, 1), 0) < own_count
    before_row = jnp.where(live_col & (place_col < place_row), 1.0, 0.0)
    order_row = jnp.where(live_row, jnp.sum(before_row, axis=0, keepdims=True).astype(I32), -1)

    def wanted(index):
        dest, number = index >> shift, index & (chunk - 1)
        return ((dest - own_offset) & (ctx - 1)) + ctx * number

    deal = one_hot(wanted(iota((slots, 1), 0)) == order_row)
    pick = one_hot(place_col == iota((cap, seq), 1))
    loads[1].wait()
    picked_rows = dot(pick, tokens_ref[...]).astype(BF16)
    row_send[...] = dot(deal, picked_rows).astype(BF16)

    pl.semaphore_wait(barrier, ctx - 1 + nx + nz - 1)

    def span(i):
        return pl.ds(pl.multiple_of(i * chunk, chunk), chunk)

    def exchange(send_ref, recv_ref, ss, rs):
        def begin(i, _):
            d = lax.rem(c + i, ctx)
            remote(
                send_ref.at[span(d)], recv_ref.at[span(c)], ss.at[d], rs.at[c], ctx=d
            ).start()
            return 0

        lax.fori_loop(1, ctx, begin, 0)
        recv_ref[span(c), :] = send_ref[span(c), :]

    def exchange_wait(send_ref, recv_ref, ss, rs):
        def end(i, _):
            d = lax.rem(c + i, ctx)
            remote(send_ref.at[span(d)], recv_ref.at[span(d)], ss.at[d], rs.at[d], ctx=d).wait()
            return 0

        lax.fori_loop(1, ctx, end, 0)

    exchange(row_send, row_recv, row_ss, row_rs)

    source = iota((8, slots), 1) >> shift
    offset_of = jnp.zeros((8, slots), I32)
    count_of = jnp.zeros((8, slots), I32)
    for i in range(ctx):
        count = counts_ref[i]
        offset_of = offset_of + jnp.where(source > i, count, 0)
        count_of = count_of + jnp.where(source == i, count, 0)
    number = ((c - offset_of) & (ctx - 1)) + ctx * (iota((8, slots), 1) & (chunk - 1))
    local_index = jnp.where(number < count_of, (offset_of + number - c) >> (ctx.bit_length() - 1), -1)
    compact = one_hot(local_index[:1] == iota((rows, slots), 0))
    spread_index = local_index.T[:, :1]
    spread = one_hot(spread_index == iota((slots, rows), 1))

    before_col = jnp.where(live_row & (place_row < place_col), 1.0, 0.0)
    order_col = jnp.where(live_col, jnp.sum(before_col, axis=1, keepdims=True).astype(I32), -1)
    undeal = one_hot(order_col == wanted(iota((1, slots), 1)))

    exchange_wait(row_send, row_recv, row_ss, row_rs)

    gathered[t, pl.ds(0, rows), :] = dot(compact, row_recv[...]).astype(BF16)
    params = jnp.concatenate(
        [
            gain_ref[...].astype(F32).reshape(1, feats),
            router_ref[...].astype(F32).reshape(1, feats),
            jnp.zeros((14, feats), F32),
        ],
        axis=0,
    )
    gathered[t, pl.ds(rows, 16), :] = params.astype(BF16)

    features = Gather(
        nx,
        x,
        core,
        lambda pos, which: gathered.at[pos * 2 + which],
        gat_ss,
        gat_rs,
        lambda pos: {"tp": pos * 2 + core},
        {"tp": sibling},
    )
    features.start()
    for step in features.steps():
        features.pass_on(step)
    for pos in range(nx):
        features.from_sibling(pos)
    features.finish()

    squares = jnp.zeros((rows, feats), F32)
    routes = jnp.zeros((rows, feats), F32)
    for b in range(tp):
        wide = gathered[b, pl.ds(0, rows), :].astype(F32)
        params = gathered[b, pl.ds(rows, 16), :].astype(F32)
        squares = squares + wide * wide
        routes = routes + wide * params[1:2]
    scale = lax.rsqrt(jnp.sum(squares, axis=1, keepdims=True) / width + EPSILON)
    gating = 1.0 / (1.0 + jnp.exp(-jnp.sum(routes, axis=1, keepdims=True)))
    for b in range(tp):
        wide = gathered[b, pl.ds(0, rows), :].astype(F32)
        params = gathered[b, pl.ds(rows, 16), :].astype(F32)
        normed_ref[:, pl.ds(b * feats, feats)] = (wide * scale * params[0:1]).astype(BF16)

    for copy in loads[2:]:
        copy.wait()
    normed = normed_ref[...]
    keys = dot(normed, wk_ref[...]).astype(BF16)
    values = dot(normed, wv_ref[...]).astype(BF16)
    for h in range(heads):
        cols = slice(h * HD, (h + 1) * HD)
        kv_send[h] = jnp.concatenate([keys[:, cols], values[:, cols]], axis=1)

    zi, parity = z // 2, lax.rem(z, 2)
    head_core = z // heads

    def to_head(h, send_ref, target, ss, rs):
        return remote(
            send_ref.at[h],
            target(zi, parity),
            ss.at[h],
            rs.at[zi],
            ctx=y * nz + heads * core + h,
            tp=x * 2 + parity,
        )

    def stays(h):
        return (heads * core + h == z) & (parity == core)

    def from_head(source, send_ref, target, ss, rs):
        return remote(
            send_ref.at[0],
            target(source, core),
            ss.at[0],
            rs.at[source],
            ctx=y * nz + source * 2 + core,
            tp=x * 2 + head_core,
        )

    def came(source):
        return (source * 2 + core == z) & (head_core == core)

    kv_target = lambda source, which: kv_ref.at[y, which, source]
    q_target = lambda source, which: q_recv.at[source]

    def deal_heads(send_ref, target, ss, rs):
        for h in range(heads):

            @pl.when(stays(h))
            def _():
                target(zi, core)[...] = send_ref[h]

            @pl.when(jnp.logical_not(stays(h)))
            def _():
                to_head(h, send_ref, target, ss, rs).start()

    def deal_heads_wait(send_ref, target, ss, rs):
        for source in range(zs):

            @pl.when(jnp.logical_not(came(source)))
            def _():
                from_head(source, send_ref, target, ss, rs).wait_recv()

    def deal_heads_sent(send_ref, target, ss, rs):
        for h in range(heads):

            @pl.when(jnp.logical_not(stays(h)))
            def _():
                to_head(h, send_ref, target, ss, rs).wait_send()

    deal_heads(kv_send, kv_target, kvz_ss, kvz_rs)

    queries = (dot(normed, wq_ref[...]).astype(BF16).astype(F32) * (1.0 / math.sqrt(HD))).astype(BF16)
    for h in range(heads):
        cols = slice(h * HD, (h + 1) * HD)
        q_send[h] = jnp.concatenate([queries[:half, cols], queries[half:, cols]], axis=1)
    deal_heads(q_send, q_target, qz_ss, qz_rs)

    def kv_view(pos, which, part):
        split = (zs + 1) // 2
        return kv_ref.at[pos, which, pl.ds(0, split) if part == 0 else pl.ds(split, zs - split)]

    blocks_kv = RingGather(
        ny,
        y,
        core,
        kv_view,
        kvy_ss,
        kvy_rs,
        lambda pos: {"ctx": pos * nz + z},
        {"tp": sibling},
        parts=2 if zs > 1 else 1,
    )
    deal_heads_wait(kv_send, kv_target, kvz_ss, kvz_rs)
    blocks_kv.start()
    deal_heads_wait(q_send, q_target, qz_ss, qz_rs)

    zeros = jnp.zeros((half, HD), BF16)
    for source in range(zs):
        packed = q_recv[source]
        q_ref[source, pl.ds(0, half), :] = jnp.concatenate([packed[:, :HD], zeros], axis=1)
        q_ref[source, pl.ds(half, half), :] = jnp.concatenate([packed[:, HD:], zeros], axis=1)

    size = rows // blocks
    tile = zs * size
    tile_row = iota((tile, 1), 0)
    tile_col = iota((1, tile), 1)
    query_key = lax.rem(tile_row, size) * ctx + y * nz + (tile_row // size) * 2 + core
    key_base = lax.rem(tile_col, size) * ctx + (tile_col // size) * 2
    value_lane = iota((1, 1, 2 * HD), 2) >= HD

    def attend(pairs, first):
        allowed = []
        for i, (pos, which) in enumerate(pairs):
            value_ref[i] = jnp.where(value_lane, kv_ref[pos, which], jnp.ones((), BF16))
            allowed.append(key_base + (pos * nz + which) <= query_key)
        for b in range(blocks):
            q = q_ref[:, pl.ds(b * size, size), :].reshape(tile, 2 * HD)
            scores, operands = [], []
            for i, (pos, which) in enumerate(pairs):
                now = pl.ds(b * size, size)
                near = kv_ref[pos, which, :, now, :].reshape(tile, 2 * HD)
                scores.append(jnp.where(allowed[i], dot_t(q, near), NEG_FILL))
                operands.append(value_ref[i, :, now, :].reshape(tile, 2 * HD))
                if b:
                    before = pl.ds(0, b * size)
                    past = kv_ref[pos, which, :, before, :].reshape(b * tile, 2 * HD)
                    scores.append(dot_t(q, past))
                    operands.append(value_ref[i, :, before, :].reshape(b * tile, 2 * HD))
            peak = None if first else max_ref[b]
            for score in scores:
                top = jnp.max(score, axis=1, keepdims=True)
                peak = top if peak is None else jnp.maximum(peak, top)
            product = None if first else acc_ref[b] * jnp.exp(max_ref[b] - peak)
            for score, operand in zip(scores, operands):
                term = dot(jnp.exp(score - peak).astype(BF16), operand)
                product = term if product is None else product + term
            max_ref[b] = peak
            acc_ref[b] = product

    blocks_kv.from_sibling(y)
    attend([(y, core), (y, 1 - core)], True)
    blocks_kv.near()
    near_by = [lax.rem(y + d, ny) for d in range(1, ny, 2)]
    far_off = [lax.rem(y + d, ny) for d in range(2, ny, 2)]
    if near_by:
        attend([(pos, core) for pos in near_by], False)
        blocks_kv.far()
        for pos in near_by:
            blocks_kv.from_sibling(pos)
        attend([(pos, 1 - core) for pos in near_by], False)
        for pos in far_off:
            blocks_kv.from_sibling(pos)
            attend([(pos, core), (pos, 1 - core)], False)
    blocks_kv.finish()
    deal_heads_sent(kv_send, kv_target, kvz_ss, kvz_rs)
    deal_heads_sent(q_send, q_target, qz_ss, qz_rs)

    for b in range(blocks):
        sums = acc_ref[b]
        result = sums[:, HD:] / sums[:, :HD]
        value_ref[0, :, pl.ds(b * size, size), :HD] = result.astype(BF16).reshape(zs, size, HD)
    for source in range(zs):
        att_send[source] = jnp.concatenate(
            [value_ref[0, source, pl.ds(0, half), :][:, :HD], value_ref[0, source, pl.ds(half, half), :][:, :HD]],
            axis=1,
        )
    own_head = lax.rem(z, heads)
    for source in range(zs):

        @pl.when(came(source))
        def _():
            att_recv[own_head] = att_send[source]

        @pl.when(jnp.logical_not(came(source)))
        def _():
            remote(
                att_send.at[source],
                att_recv.at[own_head],
                att_ss.at[source],
                att_rs.at[own_head],
                ctx=y * nz + source * 2 + core,
                tp=x * 2 + head_core,
            ).start()

    for h in range(heads):

        @pl.when(jnp.logical_not(stays(h)))
        def _():
            remote(
                att_send.at[0],
                att_recv.at[h],
                att_ss.at[0],
                att_rs.at[h],
                ctx=y * nz + heads * core + h,
                tp=x * 2 + parity,
            ).wait_recv()

    joined = [att_recv[h] for h in range(heads)]
    attended = jnp.concatenate(
        [
            jnp.concatenate([packed[:, :HD] for packed in joined], axis=1),
            jnp.concatenate([packed[:, HD:] for packed in joined], axis=1),
        ],
        axis=0,
    )

    def columns(index):
        return pl.ds(pl.multiple_of(index * feats, feats), feats)

    pair_order = [2, 1, 3, 0] if nx == 4 else [1, 0] if nx == 2 else [0]
    pair_copies = [None] * nx
    for dx in pair_order:
        other = lax.rem(x + dx, nx)
        pair_send[dx] = dot(attended, wo_ref[:, columns(other * 2 + 1 - core)]).astype(BF16)
        copy = remote(pair_send.at[dx], pair_recv.at[dx], pair_ss.at[dx], pair_rs.at[dx], tp=sibling)
        copy.start()
        pair_copies[dx] = copy
    for dx in pair_order:
        other = lax.rem(x + dx, nx)
        own_ref[dx] = dot(attended, wo_ref[:, columns(other * 2 + core)])
    part_copies = []
    for dx in pair_order[:-1]:
        other = lax.rem(x + dx, nx)
        pair_copies[dx].wait()
        part_send[dx] = (own_ref[dx] + pair_recv[dx].astype(F32)).astype(BF16)
        copy = remote(
            part_send.at[dx], part_recv.at[dx], part_ss.at[dx], part_rs.at[dx], tp=other * 2 + core
        )
        copy.start()
        part_copies.append(copy)
    pair_copies[0].wait()
    projected = own_ref[0] + pair_recv[0].astype(F32)
    for copy in reversed(part_copies):
        copy.wait()
    for dx in range(1, nx):
        projected = projected + part_recv[dx].astype(F32)
    gated = (gating * projected).astype(BF16)

    for source in range(zs):

        @pl.when(jnp.logical_not(came(source)))
        def _():
            remote(
                att_send.at[source],
                att_recv.at[own_head],
                att_ss.at[source],
                att_rs.at[own_head],
                ctx=y * nz + source * 2 + core,
                tp=x * 2 + head_core,
            ).wait_send()

    back_send[...] = dot(spread, gated).astype(BF16)
    exchange(back_send, back_recv, back_ss, back_rs)
    exchange_wait(back_send, back_recv, back_ss, back_rs)
    out_ref[...] = dot(undeal, back_recv[...]).astype(BF16)


def build(cfg, tokens, router, gain, w_query, w_key, w_value, w_out, counts, picked):
    ny, nz, nx = cfg["ny"], cfg["nz"], cfg["nx"]
    rows, chunk, blocks = cfg["rows"], cfg["chunk"], cfg["blocks"]
    ctx, tp = ny * nz, nx * 2
    feats = tokens.shape[1]
    cap = picked.shape[1]
    slots = ctx * chunk
    half = rows // 2
    width = feats * tp
    heads = feats // HD
    zs = nz // 2
    tile = zs * rows // blocks
    vmem = pl.BlockSpec(memory_space=pltpu.VMEM)
    hbm = pl.BlockSpec(memory_space=pltpu.HBM)
    dma = pltpu.SemaphoreType.DMA
    return pl.pallas_call(
        functools.partial(kernel, cfg),
        out_shape=jax.ShapeDtypeStruct((cap, feats), BF16),
        in_specs=[pl.BlockSpec(memory_space=pltpu.SMEM)] + [vmem] * 2 + [hbm] * 6,
        out_specs=vmem,
        scratch_shapes=[
            pltpu.VMEM(picked.shape, I32),
            pltpu.VMEM(tokens.shape, BF16),
            pltpu.VMEM((width, feats), BF16),
            pltpu.VMEM((width, feats), BF16),
            pltpu.VMEM((width, feats), BF16),
            pltpu.VMEM((feats, width), BF16),
            pltpu.VMEM((slots, feats), BF16),
            pltpu.VMEM((slots, feats), BF16),
            pltpu.VMEM((tp, rows + 16, feats), BF16),
            pltpu.VMEM((rows, width), BF16),
            pltpu.VMEM((heads, rows, 2 * HD), BF16),
            pltpu.VMEM((ny, 2, zs, rows, 2 * HD), BF16),
            pltpu.VMEM((heads, half, 2 * HD), BF16),
            pltpu.VMEM((zs, half, 2 * HD), BF16),
            pltpu.VMEM((zs, rows, 2 * HD), BF16),
            pltpu.VMEM((2, zs, rows, 2 * HD), BF16),
            pltpu.VMEM((blocks, tile, 1), F32),
            pltpu.VMEM((blocks, tile, 2 * HD), F32),
            pltpu.VMEM((zs, half, 2 * HD), BF16),
            pltpu.VMEM((heads, half, 2 * HD), BF16),
            pltpu.VMEM((nx, rows, feats), BF16),
            pltpu.VMEM((nx, rows, feats), BF16),
            pltpu.VMEM((nx, rows, feats), F32),
            pltpu.VMEM((nx, rows, feats), BF16),
            pltpu.VMEM((nx, rows, feats), BF16),
            pltpu.VMEM((slots, feats), BF16),
            pltpu.VMEM((slots, feats), BF16),
            dma((6,)),
            dma((ctx,)),
            dma((ctx,)),
            dma((2 * nx,)),
            dma((nx, 2)),
            dma((heads,)),
            dma((zs,)),
            dma((heads,)),
            dma((zs,)),
            dma((4 * ny + 4,)),
            dma((ny, 2, 2)),
            dma((zs,)),
            dma((heads,)),
            dma((nx,)),
            dma((nx,)),
            dma((nx,)),
            dma((nx,)),
            dma((ctx,)),
            dma((ctx,)),
        ],
        compiler_params=pltpu.CompilerParams(
            collective_id=0, has_side_effects=True, vmem_limit_bytes=VMEM_BYTES
        ),
    )(counts, gain, router, picked, tokens, w_query, w_key, w_value, w_out)


def solution(mesh, nz=8, selected=6144, cap=384, blocks=3):
    ctx, tp = mesh.shape["ctx"], mesh.shape["tp"]
    per = -(-cap // ctx)
    cfg = {
        "ny": ctx // nz,
        "nz": nz,
        "nx": tp // 2,
        "rows": selected // ctx,
        "chunk": -(-per // 16) * 16,
        "blocks": blocks,
    }
    return jax.shard_map(
        functools.partial(build, cfg),
        mesh=mesh,
        in_specs=(
            P("ctx", "tp"),
            P("tp"),
            P("tp"),
            P(None, "tp"),
            P(None, "tp"),
            P(None, "tp"),
            P("tp", None),
            P(),
            P(),
        ),
        out_specs=P("ctx", "tp"),
        check_vma=False,
    )
```

time: 89.6 us -> 78 us (0.87)
  local copies, waits for them, and re-layouts: 9.4 us -> 1.62 us
  Pallas kernels: 79.7 us -> 76.3 us
    unnamed x19 -> x1, local copies, waits for them, and re-layouts: 9.31 us -> 1.62 us
    pallas_call x1, Pallas kernels: 79.7 us -> 76.3 us  [build(): pl.pallas_call(functools.partial(kernel, cfg), out_shape=jax.ShapeDtypeSt...]
where the time goes in v2:
time: 78 us; the launch traced here: 77.9 us
  Pallas kernels  76.3 us (98%)
  local copies, waits for them, and re-layouts  1.62 us (2%)
    pallas_call x1, Pallas kernels, build(): pl.pallas_call(functools.partial(kernel, cfg), out_shape=jax.ShapeDtypeSt...  76.3 us
    unnamed x1, local copies, waits for them, and re-layouts  1.62 us

profile of v2, /device:TPU:1, one launch (start us, length us, event | category | flops | bytes accessed | tf_op | source)
XLA Modules:
  0.0 77.9 jit_solution(715518866600881209)
XLA Ops:
  0.0 76.3 %shard_map.91 = bf16[384,256]{1,0:T(8,128)(2,1)} custom-call(s32[32]{0:T(128)} %counts_ref.1, bf16[256]{0:T(256)(128)(2,1)} %gain_ref.1, bf16[256]{0:T(256)(128)(2,1)} %router_ref.1, s32[32,384]{1,0:T(8,128)} %picked_hbm.1, bf16[1536,256]{1,0:T(8,128)(2,1)} %tokens_hbm.1, bf16[2048,256]{1,0:T(8,128)(2,1)} %wq_hbm.1, bf16[2048,256]{1,0:T(8,128)(2,1)} %wk_hbm.1, ...), custom_call_target="tpu_custom_call" | custom-call | tf_op jit(solution)/shard_map/pallas_call | solution.py:637
  76.3 1.6 %copy.11 = bf16[384,256]{1,0:T(8,128)(2,1)} copy(bf16[384,256]{1,0:T(8,128)(2,1)} %shard_map.91) | data formatting | bytes 393216

commit v3 on v2

v3 whole, which is shorter than its diff:
```python
import functools
import math

import jax
import jax.numpy as jnp
from jax import lax
from jax.experimental import pallas as pl
from jax.experimental.pallas import tpu as pltpu
from jax.sharding import PartitionSpec as P

HD = 64
EPSILON = 1e-05
NEG_FILL = -1e30
MESH = pl.DeviceIdType.MESH
BF16 = jnp.bfloat16
F32 = jnp.float32
I32 = jnp.int32
VMEM_BYTES = 60 * 1024 * 1024


def iota(shape, dim):
    return lax.broadcasted_iota(I32, shape, dim)


def one_hot(mask):
    return jnp.where(mask, 1.0, 0.0).astype(BF16)


def dot(a, b):
    return jnp.dot(a, b, preferred_element_type=F32)


def dot_t(a, b):
    return lax.dot_general(a, b, (((1,), (1,)), ((), ())), preferred_element_type=F32)


def remote(src, dst, send, recv, **where):
    return pltpu.make_async_remote_copy(
        src_ref=src, dst_ref=dst, send_sem=send, recv_sem=recv, device_id=where, device_id_type=MESH
    )


class RingGather:
    def __init__(self, n, pos, core, view, ss, rs, device, sibling, parts=2):
        self.n, self.pos, self.core, self.view, self.ss, self.rs = n, pos, core, view, ss, rs
        self.device, self.sibling, self.parts = device, sibling, parts
        self.sent = []

    def at(self, step):
        return lax.rem(self.pos + step + self.n, self.n)

    def copy(self, pos, which, part, target):
        view = self.view(pos, which, part)
        return remote(view, view, self.ss(len(self.sent)), self.rs(pos, which, part), **target)

    def send(self, pos, part, target):
        copy = self.copy(pos, self.core, part, target)
        copy.start()
        self.sent.append(copy)

    def wait(self, pos, which, part):
        view = self.view(pos, which, part)
        remote(view, view, self.ss(0), self.rs(pos, which, part), **self.sibling).wait_recv()

    def start(self):
        right, left = self.device(self.at(1)), self.device(self.at(-1))
        parts = range(self.parts)
        for part in parts:
            if self.n > 1:
                self.send(self.pos, part, right)
            if self.n > 2:
                self.send(self.pos, self.parts - 1 - part, left)
        for part in parts:
            self.send(self.pos, part, self.sibling)

    def near(self):
        if self.n == 1:
            return
        right, left = self.device(self.at(1)), self.device(self.at(-1))
        for turn in range(self.parts):
            for step in (-1, 1) if self.n > 2 else (-1,):
                part = turn if step == -1 else self.parts - 1 - turn
                self.wait(self.at(step), self.core, part)
                if self.n > 2 and (turn == 0 and self.parts == 2 or self.parts == 1 and step == -1):
                    self.send(self.at(step), part, right if step == -1 else left)
                self.send(self.at(step), part, self.sibling)

    def far(self):
        if self.n > 2:
            for part in range(self.parts):
                self.wait(self.at(2), self.core, part)
                self.send(self.at(2), part, self.sibling)

    def from_sibling(self, pos):
        for part in range(self.parts):
            self.wait(pos, 1 - self.core, part)

    def finish(self):
        for copy in self.sent:
            copy.wait_send()


class Gather:
    def __init__(self, n, pos, core, view, ss, rs, device, sibling):
        self.n, self.pos, self.core, self.view, self.ss, self.rs = n, pos, core, view, ss, rs
        self.device, self.sibling = device, sibling
        self.sent = []

    def at(self, step):
        return lax.rem(self.pos + step, self.n)

    def copy(self, pos, which, slot, target):
        view = self.view(pos, which)
        return remote(view, view, self.ss(slot), self.rs(pos, which), **target)

    def send(self, pos, target):
        copy = self.copy(pos, self.core, len(self.sent), target)
        copy.start()
        self.sent.append(copy)

    def steps(self):
        return sorted(range(1, self.n), key=lambda d: min(d, self.n - d))

    def start(self):
        self.send(self.pos, self.sibling)
        for step in self.steps():
            self.send(self.pos, self.device(self.at(step)))

    def pass_on(self, step):
        self.copy(self.at(step), self.core, 0, self.sibling).wait_recv()
        self.send(self.at(step), self.sibling)

    def from_sibling(self, pos):
        self.copy(pos, 1 - self.core, 0, self.sibling).wait_recv()

    def finish(self):
        for copy in self.sent:
            copy.wait_send()


def kernel(
    cfg,
    counts_ref,
    gain_ref,
    router_ref,
    picked_hbm,
    tokens_hbm,
    wq_hbm,
    wk_hbm,
    wv_hbm,
    wo_hbm,
    out_ref,
    picked_ref,
    tokens_ref,
    wq_ref,
    wk_ref,
    wv_ref,
    wo_ref,
    row_send,
    row_recv,
    gathered,
    normed_ref,
    kv_send,
    kv_ref,
    q_send,
    q_recv,
    q_ref,
    value_ref,
    max_ref,
    acc_ref,
    done_ref,
    gated_ref,
    att_send,
    att_recv,
    pair_send,
    pair_recv,
    own_ref,
    part_send,
    part_recv,
    back_send,
    back_recv,
    w_sem,
    row_ss,
    row_rs,
    gat_ss,
    gat_rs,
    kvz_ss,
    kvz_rs,
    qz_ss,
    qz_rs,
    kvy_ss,
    kvy_rs,
    att_ss,
    att_rs,
    pair_ss,
    pair_rs,
    part_ss,
    part_rs,
    back_ss,
    back_rs,
):
    ny, nz, nx = cfg["ny"], cfg["nz"], cfg["nx"]
    rows, chunk, blocks = cfg["rows"], cfg["chunk"], cfg["blocks"]
    ctx, tp = ny * nz, nx * 2
    seq, feats = tokens_ref.shape
    cap = picked_ref.shape[1]
    slots = ctx * chunk
    shift = chunk.bit_length() - 1
    half = rows // 2
    quarter = half // 2
    width = feats * tp
    heads = feats // HD
    zs = nz // 2

    loads = [
        pltpu.make_async_copy(src, dst, w_sem.at[i])
        for i, (src, dst) in enumerate(
            (
                (picked_hbm, picked_ref),
                (tokens_hbm, tokens_ref),
                (wk_hbm, wk_ref),
                (wv_hbm, wv_ref),
                (wq_hbm, wq_ref),
                (wo_hbm, wo_ref),
            )
        )
    ]
    for copy in loads:
        copy.start()

    c = lax.axis_index("ctx")
    t = lax.axis_index("tp")
    y, z = c // nz, lax.rem(c, nz)
    x, core = t // 2, lax.rem(t, 2)
    sibling = x * 2 + 1 - core

    barrier = pltpu.get_barrier_semaphore()

    def greet(i, _):
        pl.semaphore_signal(
            barrier, inc=1, device_id={"ctx": lax.rem(c + i, ctx)}, device_id_type=MESH
        )
        return 0

    lax.fori_loop(1, ctx, greet, 0)
    for dx in range(1, nx):
        pl.semaphore_signal(
            barrier,
            inc=1,
            device_id={"tp": lax.rem(x + dx, nx) * 2 + core},
            device_id_type=MESH,
        )
    pl.semaphore_signal(barrier, inc=1, device_id={"tp": sibling}, device_id_type=MESH)
    for dz in range(1, nz):
        pl.semaphore_signal(
            barrier,
            inc=1,
            device_id={"ctx": y * nz + lax.rem(z + dz, nz), "tp": sibling},
            device_id_type=MESH,
        )

    own_count = counts_ref[c]
    own_offset = jnp.int32(0)
    for i in range(ctx):
        own_offset = own_offset + jnp.where(i < c, counts_ref[i], 0)
    loads[0].wait()
    place_row = picked_ref[pl.ds(c, 1), :] - c * seq
    place_col = jnp.broadcast_to(place_row, (8, cap)).T[:, :1]
    live_row = iota((1, cap), 1) < own_count
    live_col = iota((cap, 1), 0) < own_count
    before_row = jnp.where(live_col & (place_col < place_row), 1.0, 0.0)
    order_row = jnp.where(live_row, jnp.sum(before_row, axis=0, keepdims=True).astype(I32), -1)

    def wanted(index):
        dest, number = index >> shift, index & (chunk - 1)
        return ((dest - own_offset) & (ctx - 1)) + ctx * number

    deal = one_hot(wanted(iota((slots, 1), 0)) == order_row)
    pick = one_hot(place_col == iota((cap, seq), 1))
    loads[1].wait()
    picked_rows = dot(pick, tokens_ref[...]).astype(BF16)
    row_send[...] = dot(deal, picked_rows).astype(BF16)

    pl.semaphore_wait(barrier, ctx - 1 + nx + nz - 1)

    def span(i):
        return pl.ds(pl.multiple_of(i * chunk, chunk), chunk)

    def exchange(send_ref, recv_ref, ss, rs):
        def begin(i, _):
            d = lax.rem(c + i, ctx)
            remote(
                send_ref.at[span(d)], recv_ref.at[span(c)], ss.at[d], rs.at[c], ctx=d
            ).start()
            return 0

        lax.fori_loop(1, ctx, begin, 0)
        recv_ref[span(c), :] = send_ref[span(c), :]

    def exchange_wait(send_ref, recv_ref, ss, rs):
        def end(i, _):
            d = lax.rem(c + i, ctx)
            remote(send_ref.at[span(d)], recv_ref.at[span(d)], ss.at[d], rs.at[d], ctx=d).wait()
            return 0

        lax.fori_loop(1, ctx, end, 0)

    exchange(row_send, row_recv, row_ss, row_rs)

    source = iota((8, slots), 1) >> shift
    offset_of = jnp.zeros((8, slots), I32)
    count_of = jnp.zeros((8, slots), I32)
    for i in range(ctx):
        count = counts_ref[i]
        offset_of = offset_of + jnp.where(source > i, count, 0)
        count_of = count_of + jnp.where(source == i, count, 0)
    number = ((c - offset_of) & (ctx - 1)) + ctx * (iota((8, slots), 1) & (chunk - 1))
    local_index = jnp.where(number < count_of, (offset_of + number - c) >> (ctx.bit_length() - 1), -1)
    compact = one_hot(local_index[:1] == iota((rows, slots), 0))
    spread_index = local_index.T[:, :1]
    spread = one_hot(spread_index == iota((slots, rows), 1))

    before_col = jnp.where(live_row & (place_row < place_col), 1.0, 0.0)
    order_col = jnp.where(live_col, jnp.sum(before_col, axis=1, keepdims=True).astype(I32), -1)
    undeal = one_hot(order_col == wanted(iota((1, slots), 1)))

    exchange_wait(row_send, row_recv, row_ss, row_rs)

    packed_rows = dot(compact, row_recv[...]).astype(BF16)
    params = jnp.concatenate(
        [
            gain_ref[...].astype(F32).reshape(1, feats),
            router_ref[...].astype(F32).reshape(1, feats),
            jnp.zeros((14, feats), F32),
        ],
        axis=0,
    )
    gathered[0, t, pl.ds(0, half), :] = packed_rows[:half]
    gathered[0, t, pl.ds(half, 16), :] = params.astype(BF16)
    gathered[1, t, pl.ds(0, half), :] = packed_rows[half:]

    def feature_gather(p):
        height = half + 16 if p == 0 else half
        return Gather(
            nx,
            x,
            core,
            lambda pos, which: gathered.at[p, pos * 2 + which, pl.ds(0, height), :],
            lambda slot: gat_ss.at[p, slot],
            lambda pos, which: gat_rs.at[p, pos, which],
            lambda pos: {"tp": pos * 2 + core},
            {"tp": sibling},
        )

    features = [feature_gather(0), feature_gather(1)]
    features[0].start()
    features[1].start()

    zi, parity = z // 2, lax.rem(z, 2)
    head_core = z // heads
    own_head = lax.rem(z, heads)

    def stays(h):
        return (heads * core + h == z) & (parity == core)

    def came(source):
        return (source * 2 + core == z) & (head_core == core)

    def to_head(h, src, dst, ss, rs):
        return remote(src, dst, ss, rs, ctx=y * nz + heads * core + h, tp=x * 2 + parity)

    def to_source(source, src, dst, ss, rs):
        return remote(src, dst, ss, rs, ctx=y * nz + source * 2 + core, tp=x * 2 + head_core)

    def kv_at(p, source, which):
        return kv_ref.at[y, which, p, source]

    def q_at(p, source, which):
        return q_recv.at[p, source]

    def deal_heads(p, send_ref, target, ss, rs):
        for h in range(heads):

            @pl.when(stays(h))
            def _():
                target(p, zi, core)[...] = send_ref[p, h]

            @pl.when(jnp.logical_not(stays(h)))
            def _():
                to_head(h, send_ref.at[p, h], target(p, zi, parity), ss.at[p, h], rs.at[p, zi]).start()

    def deal_heads_wait(p, send_ref, target, ss, rs):
        for source in range(zs):

            @pl.when(jnp.logical_not(came(source)))
            def _():
                to_source(
                    source, send_ref.at[p, 0], target(p, source, core), ss.at[p, 0], rs.at[p, source]
                ).wait_recv()

    def deal_heads_sent(p, send_ref, target, ss, rs):
        for h in range(heads):

            @pl.when(jnp.logical_not(stays(h)))
            def _():
                to_head(h, send_ref.at[p, h], target(p, zi, parity), ss.at[p, h], rs.at[p, zi]).wait_send()

    def project(p):
        squares = jnp.zeros((half, feats), F32)
        routes = jnp.zeros((half, feats), F32)
        for b in range(tp):
            wide = gathered[p, b, pl.ds(0, half), :].astype(F32)
            params = gathered[0, b, pl.ds(half, 16), :].astype(F32)
            squares = squares + wide * wide
            routes = routes + wide * params[1:2]
        scale = lax.rsqrt(jnp.sum(squares, axis=1, keepdims=True) / width + EPSILON)
        for b in range(tp):
            wide = gathered[p, b, pl.ds(0, half), :].astype(F32)
            params = gathered[0, b, pl.ds(half, 16), :].astype(F32)
            normed_ref[p, :, pl.ds(b * feats, feats)] = (wide * scale * params[0:1]).astype(BF16)
        normed = normed_ref[p]
        keys = dot(normed, wk_ref[...]).astype(BF16)
        values = dot(normed, wv_ref[...]).astype(BF16)
        for h in range(heads):
            cols = slice(h * HD, (h + 1) * HD)
            kv_send[p, h] = jnp.concatenate([keys[:, cols], values[:, cols]], axis=1)
        deal_heads(p, kv_send, kv_at, kvz_ss, kvz_rs)
        queries = (dot(normed, wq_ref[...]).astype(BF16).astype(F32) * (1.0 / math.sqrt(HD))).astype(BF16)
        for h in range(heads):
            cols = slice(h * HD, (h + 1) * HD)
            q_send[p, h] = jnp.concatenate([queries[:quarter, cols], queries[quarter:, cols]], axis=1)
        deal_heads(p, q_send, q_at, qz_ss, qz_rs)
        return 1.0 / (1.0 + jnp.exp(-jnp.sum(routes, axis=1, keepdims=True)))

    def gather_end(p):
        for step in features[p].steps():
            features[p].pass_on(step)
        for pos in range(nx):
            features[p].from_sibling(pos)

    gather_end(0)
    for copy in loads[2:]:
        copy.wait()
    gating = [project(0)]
    gather_end(1)
    gating.append(project(1))

    kv_parts = 2 if zs > 1 else 1

    def kv_gather(p):
        split = (zs + 1) // 2
        return RingGather(
            ny,
            y,
            core,
            lambda pos, which, part: kv_ref.at[
                pos, which, p, pl.ds(0, split) if part == 0 else pl.ds(split, zs - split)
            ],
            lambda slot: kvy_ss.at[p, slot],
            lambda pos, which, part: kvy_rs.at[p, pos, which, part],
            lambda pos: {"ctx": pos * nz + z},
            {"tp": sibling},
            parts=kv_parts,
        )

    blocks_kv = [kv_gather(0), kv_gather(1)]
    size = half // blocks
    tile = zs * size
    tile_row = iota((tile, 1), 0)
    tile_col = iota((1, tile), 1)
    query_key = lax.rem(tile_row, size) * ctx + y * nz + (tile_row // size) * 2 + core
    key_base = lax.rem(tile_col, size) * ctx + (tile_col // size) * 2
    value_lane = iota((1, 1, 2 * HD), 2) >= HD
    zeros = jnp.zeros((quarter, HD), BF16)

    def queries_in(p):
        deal_heads_wait(p, q_send, q_at, qz_ss, qz_rs)
        for source in range(zs):
            packed = q_recv[p, source]
            q_ref[p, source, pl.ds(0, quarter), :] = jnp.concatenate([packed[:, :HD], zeros], axis=1)
            q_ref[p, source, pl.ds(quarter, quarter), :] = jnp.concatenate([packed[:, HD:], zeros], axis=1)

    def attend(p, pairs, first=False):
        allowed = []
        for pos, which in pairs:
            value_ref[pos, which, p] = jnp.where(value_lane, kv_ref[pos, which, p], jnp.ones((), BF16))
            allowed.append(key_base + (pos * nz + which) <= query_key)
        for b in range(blocks):
            now = pl.ds(b * size, size)
            q = q_ref[p, :, now, :].reshape(tile, 2 * HD)
            scores, operands = [], []
            for i, (pos, which) in enumerate(pairs):
                near = kv_ref[pos, which, p, :, now, :].reshape(tile, 2 * HD)
                scores.append(jnp.where(allowed[i], dot_t(q, near), NEG_FILL))
                operands.append(value_ref[pos, which, p, :, now, :].reshape(tile, 2 * HD))
                if b:
                    before = pl.ds(0, b * size)
                    past = kv_ref[pos, which, p, :, before, :].reshape(b * tile, 2 * HD)
                    scores.append(dot_t(q, past))
                    operands.append(value_ref[pos, which, p, :, before, :].reshape(b * tile, 2 * HD))
                if p:
                    scores.append(dot_t(q, kv_ref[pos, which, 0].reshape(zs * half, 2 * HD)))
                    operands.append(value_ref[pos, which, 0].reshape(zs * half, 2 * HD))
            peak = None if first else max_ref[p, b]
            for score in scores:
                top = jnp.max(score, axis=1, keepdims=True)
                peak = top if peak is None else jnp.maximum(peak, top)
            product = None if first else acc_ref[p, b] * jnp.exp(max_ref[p, b] - peak)
            for score, operand in zip(scores, operands):
                term = dot(jnp.exp(score - peak).astype(BF16), operand)
                product = term if product is None else product + term
            max_ref[p, b] = peak
            acc_ref[p, b] = product

    def back_start(p):
        for b in range(blocks):
            sums = acc_ref[p, b]
            result = sums[:, HD:] / sums[:, :HD]
            done_ref[p, :, pl.ds(b * size, size), :] = result.astype(BF16).reshape(zs, size, HD)
        for source in range(zs):
            att_send[p, source] = jnp.concatenate(
                [done_ref[p, source, pl.ds(0, quarter), :], done_ref[p, source, pl.ds(quarter, quarter), :]], axis=1
            )
        for source in range(zs):

            @pl.when(came(source))
            def _():
                att_recv[p, own_head] = att_send[p, source]

            @pl.when(jnp.logical_not(came(source)))
            def _():
                back_copy(p, source).start()

    def back_copy(p, source):
        return to_source(
            source, att_send.at[p, source], att_recv.at[p, own_head], att_ss.at[p, source], att_rs.at[p, own_head]
        )

    def back_wait(p):
        for h in range(heads):

            @pl.when(jnp.logical_not(stays(h)))
            def _():
                to_head(h, att_send.at[p, 0], att_recv.at[p, h], att_ss.at[p, 0], att_rs.at[p, h]).wait_recv()

    def columns(index):
        return pl.ds(pl.multiple_of(index * feats, feats), feats)

    pair_order = [2, 1, 3, 0] if nx == 4 else [1, 0] if nx == 2 else [0]
    pair_copies = [[None] * nx, [None] * nx]
    part_copies = [[], []]

    def pair_sums(p):
        joined = [att_recv[p, h] for h in range(heads)]
        attended = jnp.concatenate(
            [
                jnp.concatenate([packed[:, :HD] for packed in joined], axis=1),
                jnp.concatenate([packed[:, HD:] for packed in joined], axis=1),
            ],
            axis=0,
        )
        for dx in pair_order:
            other = lax.rem(x + dx, nx)
            pair_send[p, dx] = dot(attended, wo_ref[:, columns(other * 2 + 1 - core)]).astype(BF16)
            copy = remote(
                pair_send.at[p, dx], pair_recv.at[p, dx], pair_ss.at[p, dx], pair_rs.at[p, dx], tp=sibling
            )
            copy.start()
            pair_copies[p][dx] = copy
        for dx in pair_order:
            other = lax.rem(x + dx, nx)
            own_ref[p, dx] = dot(attended, wo_ref[:, columns(other * 2 + core)])

    def part_sums(p):
        for dx in pair_order[:-1]:
            other = lax.rem(x + dx, nx)
            pair_copies[p][dx].wait()
            part_send[p, dx] = (own_ref[p, dx] + pair_recv[p, dx].astype(F32)).astype(BF16)
            copy = remote(
                part_send.at[p, dx], part_recv.at[p, dx], part_ss.at[p, dx], part_rs.at[p, dx], tp=other * 2 + core
            )
            copy.start()
            part_copies[p].append(copy)

    def finish_rows(p):
        pair_copies[p][0].wait()
        projected = own_ref[p, 0] + pair_recv[p, 0].astype(F32)
        for copy in part_copies[p]:
            copy.wait()
        for dx in range(1, nx):
            projected = projected + part_recv[p, dx].astype(F32)
        gated_ref[pl.ds(p * half, half), :] = (gating[p] * projected).astype(BF16)

    near_by = [lax.rem(y + d, ny) for d in range(1, ny, 2)]
    far_off = [lax.rem(y + d, ny) for d in range(2, ny, 2)]

    def keys_in(p):
        deal_heads_wait(p, kv_send, kv_at, kvz_ss, kvz_rs)
        blocks_kv[p].start()

    def attend_own(p):
        blocks_kv[p].from_sibling(y)
        attend(p, [(y, core), (y, 1 - core)], True)

    def attend_near(p):
        if near_by:
            attend(p, [(pos, core) for pos in near_by])

    def attend_near_other(p):
        if near_by:
            for pos in near_by:
                blocks_kv[p].from_sibling(pos)
            attend(p, [(pos, 1 - core) for pos in near_by])

    def attend_far(p):
        for pos in far_off:
            blocks_kv[p].from_sibling(pos)
            attend(p, [(pos, core), (pos, 1 - core)])

    keys_in(0)
    queries_in(0)
    attend_own(0)
    keys_in(1)
    blocks_kv[0].near()
    attend_near(0)
    queries_in(1)
    attend_own(1)
    blocks_kv[0].far()
    attend_near_other(0)
    blocks_kv[1].near()
    attend_far(0)
    back_start(0)
    attend_near(1)
    blocks_kv[1].far()
    attend_near_other(1)
    back_wait(0)
    pair_sums(0)
    attend_far(1)
    back_start(1)
    part_sums(0)
    back_wait(1)
    pair_sums(1)
    part_sums(1)
    finish_rows(0)
    finish_rows(1)

    back_send[...] = dot(spread, gated_ref[...]).astype(BF16)
    exchange(back_send, back_recv, back_ss, back_rs)
    for p in (0, 1):
        features[p].finish()
        blocks_kv[p].finish()
        deal_heads_sent(p, kv_send, kv_at, kvz_ss, kvz_rs)
        deal_heads_sent(p, q_send, q_at, qz_ss, qz_rs)
        for source in range(zs):

            @pl.when(jnp.logical_not(came(source)))
            def _():
                back_copy(p, source).wait_send()

    exchange_wait(back_send, back_recv, back_ss, back_rs)
    out_ref[...] = dot(undeal, back_recv[...]).astype(BF16)


def build(cfg, tokens, router, gain, w_query, w_key, w_value, w_out, counts, picked):
    ny, nz, nx = cfg["ny"], cfg["nz"], cfg["nx"]
    rows, chunk, blocks = cfg["rows"], cfg["chunk"], cfg["blocks"]
    ctx, tp = ny * nz, nx * 2
    feats = tokens.shape[1]
    cap = picked.shape[1]
    slots = ctx * chunk
    half = rows // 2
    width = feats * tp
    heads = feats // HD
    zs = nz // 2
    tile = zs * (half // blocks)
    vmem = pl.BlockSpec(memory_space=pltpu.VMEM)
    hbm = pl.BlockSpec(memory_space=pltpu.HBM)
    dma = pltpu.SemaphoreType.DMA
    return pl.pallas_call(
        functools.partial(kernel, cfg),
        out_shape=jax.ShapeDtypeStruct((cap, feats), BF16),
        in_specs=[pl.BlockSpec(memory_space=pltpu.SMEM)] + [vmem] * 2 + [hbm] * 6,
        out_specs=vmem,
        scratch_shapes=[
            pltpu.VMEM(picked.shape, I32),
            pltpu.VMEM(tokens.shape, BF16),
            pltpu.VMEM((width, feats), BF16),
            pltpu.VMEM((width, feats), BF16),
            pltpu.VMEM((width, feats), BF16),
            pltpu.VMEM((feats, width), BF16),
            pltpu.VMEM((slots, feats), BF16),
            pltpu.VMEM((slots, feats), BF16),
            pltpu.VMEM((2, tp, half + 16, feats), BF16),
            pltpu.VMEM((2, half, width), BF16),
            pltpu.VMEM((2, heads, half, 2 * HD), BF16),
            pltpu.VMEM((ny, 2, 2, zs, half, 2 * HD), BF16),
            pltpu.VMEM((2, heads, half // 2, 2 * HD), BF16),
            pltpu.VMEM((2, zs, half // 2, 2 * HD), BF16),
            pltpu.VMEM((2, zs, half, 2 * HD), BF16),
            pltpu.VMEM((ny, 2, 2, zs, half, 2 * HD), BF16),
            pltpu.VMEM((2, blocks, tile, 1), F32),
            pltpu.VMEM((2, blocks, tile, 2 * HD), F32),
            pltpu.VMEM((2, zs, half, HD), BF16),
            pltpu.VMEM((rows, feats), BF16),
            pltpu.VMEM((2, zs, half // 2, 2 * HD), BF16),
            pltpu.VMEM((2, heads, half // 2, 2 * HD), BF16),
            pltpu.VMEM((2, nx, half, feats), BF16),
            pltpu.VMEM((2, nx, half, feats), BF16),
            pltpu.VMEM((2, nx, half, feats), F32),
            pltpu.VMEM((2, nx, half, feats), BF16),
            pltpu.VMEM((2, nx, half, feats), BF16),
            pltpu.VMEM((slots, feats), BF16),
            pltpu.VMEM((slots, feats), BF16),
            dma((6,)),
            dma((ctx,)),
            dma((ctx,)),
            dma((2, 2 * nx)),
            dma((2, nx, 2)),
            dma((2, heads)),
            dma((2, zs)),
            dma((2, heads)),
            dma((2, zs)),
            dma((2, 4 * ny + 4)),
            dma((2, ny, 2, 2)),
            dma((2, zs)),
            dma((2, heads)),
            dma((2, nx)),
            dma((2, nx)),
            dma((2, nx)),
            dma((2, nx)),
            dma((ctx,)),
            dma((ctx,)),
        ],
        compiler_params=pltpu.CompilerParams(
            collective_id=0, has_side_effects=True, vmem_limit_bytes=VMEM_BYTES
        ),
    )(counts, gain, router, picked, tokens, w_query, w_key, w_value, w_out)


def solution(mesh, nz=8, selected=6144, cap=384, blocks=1):
    ctx, tp = mesh.shape["ctx"], mesh.shape["tp"]
    per = -(-cap // ctx)
    cfg = {
        "ny": ctx // nz,
        "nz": nz,
        "nx": tp // 2,
        "rows": selected // ctx,
        "chunk": -(-per // 16) * 16,
        "blocks": blocks,
    }
    return jax.shard_map(
        functools.partial(build, cfg),
        mesh=mesh,
        in_specs=(
            P("ctx", "tp"),
            P("tp"),
            P("tp"),
            P(None, "tp"),
            P(None, "tp"),
            P(None, "tp"),
            P("tp", None),
            P(),
            P(),
        ),
        out_specs=P("ctx", "tp"),
        check_vma=False,
    )
```

time: 78 us -> 75.9 us (0.973)
  Pallas kernels: 76.3 us -> 74.2 us
    pallas_call x1, Pallas kernels: 76.3 us -> 74.2 us  [build(): pl.pallas_call(functools.partial(kernel, cfg), out_shape=jax.ShapeDtypeSt...]
where the time goes in v3:
time: 75.9 us; the launch traced here: 75.8 us
  Pallas kernels  74.2 us (98%)
  local copies, waits for them, and re-layouts  1.62 us (2%)
    pallas_call x1, Pallas kernels, build(): pl.pallas_call(functools.partial(kernel, cfg), out_shape=jax.ShapeDtypeSt...  74.2 us
    unnamed x1, local copies, waits for them, and re-layouts  1.62 us

profile of v3, /device:TPU:1, one launch (start us, length us, event | category | flops | bytes accessed | tf_op | source)
XLA Modules:
  0.0 75.8 jit_solution(10715361116867374250)
XLA Ops:
  0.0 74.2 %shard_map.91 = bf16[384,256]{1,0:T(8,128)(2,1)} custom-call(s32[32]{0:T(128)} %counts_ref.1, bf16[256]{0:T(256)(128)(2,1)} %gain_ref.1, bf16[256]{0:T(256)(128)(2,1)} %router_ref.1, s32[32,384]{1,0:T(8,128)} %picked_hbm.1, bf16[1536,256]{1,0:T(8,128)(2,1)} %tokens_hbm.1, bf16[2048,256]{1,0:T(8,128)(2,1)} %wq_hbm.1, bf16[2048,256]{1,0:T(8,128)(2,1)} %wk_hbm.1, ...), custom_call_target="tpu_custom_call" | custom-call | tf_op jit(solution)/shard_map/pallas_call | solution.py:679
  74.2 1.6 %copy.11 = bf16[384,256]{1,0:T(8,128)(2,1)} copy(bf16[384,256]{1,0:T(8,128)(2,1)} %shard_map.91) | data formatting | bytes 393216

commit v4 on v3

--- a/solution.py
+++ b/solution.py
@@ -633,10 +633,10 @@
     attend_near(1)
     blocks_kv[1].far()
     attend_near_other(1)
+    attend_far(1)
+    back_start(1)
     back_wait(0)
     pair_sums(0)
-    attend_far(1)
-    back_start(1)
     part_sums(0)
     back_wait(1)
     pair_sums(1)

time: 75.9 us -> 73.6 us (0.970)
  Pallas kernels: 74.2 us -> 71.9 us
    pallas_call x1, Pallas kernels: 74.2 us -> 71.9 us  [build(): pl.pallas_call(functools.partial(kernel, cfg), out_shape=jax.ShapeDtypeSt...]
where the time goes in v4:
time: 73.6 us; the launch traced here: 73.5 us
  Pallas kernels  71.9 us (98%)
  local copies, waits for them, and re-layouts  1.62 us (2%)
    pallas_call x1, Pallas kernels, build(): pl.pallas_call(functools.partial(kernel, cfg), out_shape=jax.ShapeDtypeSt...  71.9 us
    unnamed x1, local copies, waits for them, and re-layouts  1.62 us

profile of v4, /device:TPU:1, one launch (start us, length us, event | category | flops | bytes accessed | tf_op | source)
XLA Modules:
  0.0 73.5 jit_solution(14406178319157404728)
XLA Ops:
  0.0 71.9 %shard_map.91 = bf16[384,256]{1,0:T(8,128)(2,1)} custom-call(s32[32]{0:T(128)} %counts_ref.1, bf16[256]{0:T(256)(128)(2,1)} %gain_ref.1, bf16[256]{0:T(256)(128)(2,1)} %router_ref.1, s32[32,384]{1,0:T(8,128)} %picked_hbm.1, bf16[1536,256]{1,0:T(8,128)(2,1)} %tokens_hbm.1, bf16[2048,256]{1,0:T(8,128)(2,1)} %wq_hbm.1, bf16[2048,256]{1,0:T(8,128)(2,1)} %wk_hbm.1, ...), custom_call_target="tpu_custom_call" | custom-call | tf_op jit(solution)/shard_map/pallas_call | solution.py:679
  71.9 1.6 %copy.11 = bf16[384,256]{1,0:T(8,128)(2,1)} copy(bf16[384,256]{1,0:T(8,128)(2,1)} %shard_map.91) | data formatting | bytes 393216

commit v5 on v4

--- a/solution.py
+++ b/solution.py
@@ -622,12 +622,12 @@
     attend_own(0)
     keys_in(1)
     blocks_kv[0].near()
+    queries_in(1)
     attend_near(0)
-    queries_in(1)
     attend_own(1)
     blocks_kv[0].far()
+    blocks_kv[1].near()
     attend_near_other(0)
-    blocks_kv[1].near()
     attend_far(0)
     back_start(0)
     attend_near(1)

time: 73.6 us -> 72.8 us (0.989)
  Pallas kernels: 71.9 us -> 71.1 us
    pallas_call x1, Pallas kernels: 71.9 us -> 71.1 us  [build(): pl.pallas_call(functools.partial(kernel, cfg), out_shape=jax.ShapeDtypeSt...]
where the time goes in v5:
time: 72.8 us; the launch traced here: 72.7 us
  Pallas kernels  71.1 us (98%)
  local copies, waits for them, and re-layouts  1.62 us (2%)
    pallas_call x1, Pallas kernels, build(): pl.pallas_call(functools.partial(kernel, cfg), out_shape=jax.ShapeDtypeSt...  71.1 us
    unnamed x1, local copies, waits for them, and re-layouts  1.62 us

profile of v5, /device:TPU:1, one launch (start us, length us, event | category | flops | bytes accessed | tf_op | source)
XLA Modules:
  0.0 72.7 jit_solution(14388330152043989559)
XLA Ops:
  0.0 71.1 %shard_map.91 = bf16[384,256]{1,0:T(8,128)(2,1)} custom-call(s32[32]{0:T(128)} %counts_ref.1, bf16[256]{0:T(256)(128)(2,1)} %gain_ref.1, bf16[256]{0:T(256)(128)(2,1)} %router_ref.1, s32[32,384]{1,0:T(8,128)} %picked_hbm.1, bf16[1536,256]{1,0:T(8,128)(2,1)} %tokens_hbm.1, bf16[2048,256]{1,0:T(8,128)(2,1)} %wq_hbm.1, bf16[2048,256]{1,0:T(8,128)(2,1)} %wk_hbm.1, ...), custom_call_target="tpu_custom_call" | custom-call | tf_op jit(solution)/shard_map/pallas_call | solution.py:679
  71.1 1.6 %copy.11 = bf16[384,256]{1,0:T(8,128)(2,1)} copy(bf16[384,256]{1,0:T(8,128)(2,1)} %shard_map.91) | data formatting | bytes 393216

commit v6 on v5

--- a/solution.py
+++ b/solution.py
@@ -619,8 +619,8 @@
 
     keys_in(0)
     queries_in(0)
+    keys_in(1)
     attend_own(0)
-    keys_in(1)
     blocks_kv[0].near()
     queries_in(1)
     attend_near(0)

time: 72.8 us -> 72.8 us (level)
  no operation moved by 1% of the time
where the time goes in v6:
time: 72.8 us; the launch traced here: 72.7 us
  Pallas kernels  71 us (98%)
  local copies, waits for them, and re-layouts  1.62 us (2%)
    pallas_call x1, Pallas kernels, build(): pl.pallas_call(functools.partial(kernel, cfg), out_shape=jax.ShapeDtypeSt...  71 us
    unnamed x1, local copies, waits for them, and re-layouts  1.62 us

profile of v6, /device:TPU:1, one launch (start us, length us, event | category | flops | bytes accessed | tf_op | source)
XLA Modules:
  0.0 72.7 jit_solution(8606573573114041430)
XLA Ops:
  0.0 71.0 %shard_map.91 = bf16[384,256]{1,0:T(8,128)(2,1)} custom-call(s32[32]{0:T(128)} %counts_ref.1, bf16[256]{0:T(256)(128)(2,1)} %gain_ref.1, bf16[256]{0:T(256)(128)(2,1)} %router_ref.1, s32[32,384]{1,0:T(8,128)} %picked_hbm.1, bf16[1536,256]{1,0:T(8,128)(2,1)} %tokens_hbm.1, bf16[2048,256]{1,0:T(8,128)(2,1)} %wq_hbm.1, bf16[2048,256]{1,0:T(8,128)(2,1)} %wk_hbm.1, ...), custom_call_target="tpu_custom_call" | custom-call | tf_op jit(solution)/shard_map/pallas_call | solution.py:679
  71.0 1.6 %copy.11 = bf16[384,256]{1,0:T(8,128)(2,1)} copy(bf16[384,256]{1,0:T(8,128)(2,1)} %shard_map.91) | data formatting | bytes 393216
